TPU v7x, 256 devices: a whole 4x4x8 slice. The times are simulated.
256 devices in a mesh: gx: 32 (over z, x), gy: 8 (over y, core).
Axes of the slice: x: 4, y: 4, z: 8, core: 2. Of those that a mesh axis runs over, the one named last changes fastest.
Arguments:
- state_field: float32 [4, 1024, 4096], P(None, 'gx', 'gy'), may hold values from -4 to 4
- x_coupling: bfloat16 [4, 1024, 4096], P(None, 'gx', 'gy'), may hold values from 9984 to 99840
- y_coupling: bfloat16 [4, 1024, 4096], P(None, 'gx', 'gy'), may hold values from 0.049804688 to 0.5
- cross_coeff: bfloat16 [4, 1024, 4096], P(None, 'gx', 'gy'), may hold values from -0.29882812 to 0.29882812
Outputs:
- solved_field: float32 [4, 1024, 4096], P(None, 'gx', 'gy')
- right_side: float32 [4, 1024, 4096], P(None, 'gx', 'gy')
All inputs are finite; a program needn't handle non-finite values.
Results may differ from a plain program's by a relative error of at most 0.0009.
Values sent between devices are 32-bit elements; how exact they have to be, the bound alone decides.
A program may use at most 64 MiB of HBM per device.

v0:
```python
import jax
import jax.numpy as jnp
from jax import lax
from jax.sharding import PartitionSpec as P


def extended(array, sides, width):
    for axis, dim in sides:
        count, length = (lax.axis_size(axis), array.shape[dim])
        up = [(i, (i + 1) % count) for i in range(count - 1)]
        down = [(j, i) for i, j in up]
        last = lax.slice_in_dim(array, length - width, length, axis=dim)
        leading = lax.slice_in_dim(array, 0, width, axis=dim)
        before = lax.ppermute(last, axis, up)
        after = lax.ppermute(leading, axis, down)
        array = jnp.concatenate([before, array, after], axis=dim)
    return array


def passed_along(value, axis, steps):
    count = lax.axis_size(axis)
    leading, last = (max(0, -steps), min(count, count - steps))
    return lax.ppermute(value, axis, [(source, source + steps) for source in range(leading, last)])


def move_rows(values, stride, fill_value, from_later):
    row_count = values.shape[-2]
    filler = jnp.full(values.shape[:-2] + (stride, values.shape[-1]), fill_value, values.dtype)
    if from_later:
        return jnp.concatenate([values[..., stride:, :], filler], axis=-2)
    return jnp.concatenate([filler, values[..., : row_count - stride, :]], axis=-2)


def cyclic_solve(lower_band, center_band, upper_band, sources):
    row_count = center_band.shape[-2]
    stride = 1
    while stride < row_count:
        low_prev = move_rows(lower_band, stride, 0.0, False)
        cen_prev = move_rows(center_band, stride, 1.0, False)
        upp_prev = move_rows(upper_band, stride, 0.0, False)
        src_prev = move_rows(sources, stride, 0.0, False)
        low_next = move_rows(lower_band, stride, 0.0, True)
        cen_next = move_rows(center_band, stride, 1.0, True)
        upp_next = move_rows(upper_band, stride, 0.0, True)
        src_next = move_rows(sources, stride, 0.0, True)
        factor_prev = -lower_band / cen_prev
        factor_next = -upper_band / cen_next
        center_band = center_band + factor_prev * upp_prev + factor_next * low_next
        sources = sources + factor_prev * src_prev + factor_next * src_next
        lower_band = factor_prev * low_prev
        upper_band = factor_next * upp_next
        stride = stride * 2
    return sources / center_band


def shards(state_field, x_coupling, y_coupling, cross_coeff):
    planes = state_field.shape[0]
    row_total = state_field.shape[1]
    x_local = x_coupling.astype(jnp.float32)
    y_local = y_coupling.astype(jnp.float32)
    stacked = jnp.concatenate([state_field, x_local, y_local], axis=0)
    padded = extended(stacked, (("gx", 1), ("gy", 2)), 1)
    state_pad = padded[:planes]
    x_pad = padded[planes : 2 * planes]
    y_pad = padded[2 * planes :]
    y_before = y_pad[:, 1:-1, :-2]
    second_y = y_local * (state_pad[:, 1:-1, 2:] - state_field) - y_before * (
        state_field - state_pad[:, 1:-1, :-2]
    )
    mixed_term = (
        cross_coeff.astype(jnp.float32)
        * (
            state_pad[:, 2:, 2:]
            - state_pad[:, 2:, :-2]
            - state_pad[:, :-2, 2:]
            + state_pad[:, :-2, :-2]
        )
        * 0.25
    )
    right_side = state_field + second_y + mixed_term
    x_before = x_pad[:, :-2, 1:-1]
    lower_band = -x_before
    center_band = 1.0 + x_before + x_local
    upper_band = -x_local
    inner_rows = row_total - 1
    zero_row = jnp.zeros_like(lower_band[:, :1])
    inner_lower = jnp.concatenate([zero_row, lower_band[:, 1:inner_rows]], axis=1)
    inner_upper = jnp.concatenate([upper_band[:, : inner_rows - 1], zero_row], axis=1)
    inner_center = center_band[:, :inner_rows]
    first_source = jnp.concatenate(
        [lower_band[:, :1], jnp.zeros_like(lower_band[:, 1:inner_rows])], axis=1
    )
    last_source = jnp.concatenate(
        [
            jnp.zeros_like(upper_band[:, : inner_rows - 1]),
            upper_band[:, inner_rows - 1 : inner_rows],
        ],
        axis=1,
    )
    sources = jnp.stack([right_side[:, :inner_rows], first_source, last_source])
    solved = cyclic_solve(inner_lower, inner_center, inner_upper, sources)
    base_part = solved[0]
    spike_prev = solved[1]
    spike_next = solved[2]
    head_rows = jnp.stack([base_part[:, 0], spike_prev[:, 0], spike_next[:, 0]])
    from_next = passed_along(head_rows, "gx", -1)
    low_last = lower_band[:, row_total - 1]
    cen_last = center_band[:, row_total - 1]
    upp_last = upper_band[:, row_total - 1]
    src_last = right_side[:, row_total - 1]
    row_lower = -low_last * spike_prev[:, -1]
    row_center = cen_last - low_last * spike_next[:, -1] - upp_last * from_next[1]
    row_upper = -upp_last * from_next[2]
    row_source = src_last - low_last * base_part[:, -1] - upp_last * from_next[0]
    system = jnp.stack([row_lower, row_center, row_upper, row_source])[:, :, None, :]
    gathered = lax.all_gather(system, "gx", axis=2, tiled=True)
    reduced_values = cyclic_solve(gathered[0], gathered[1], gathered[2], gathered[3][None])[0]
    padded_values = jnp.concatenate([jnp.zeros_like(reduced_values[:, :1]), reduced_values], axis=1)
    own_index = lax.axis_index("gx")
    value_prev = lax.dynamic_index_in_dim(padded_values, own_index, 1, keepdims=False)
    value_own = lax.dynamic_index_in_dim(padded_values, own_index + 1, 1, keepdims=False)
    interior = base_part - spike_prev * value_prev[:, None, :] - spike_next * value_own[:, None, :]
    solved_field = jnp.concatenate([interior, value_own[:, None, :]], axis=1)
    return (solved_field, right_side)


def solution(mesh):
    return jax.shard_map(
        shards,
        mesh=mesh,
        in_specs=(
            P(None, "gx", "gy"),
            P(None, "gx", "gy"),
            P(None, "gx", "gy"),
            P(None, "gx", "gy"),
        ),
        out_specs=(P(None, "gx", "gy"), P(None, "gx", "gy")),
        check_vma=False,
    )
```

profile of v0, /device:TPU:8, one launch (start us, length us, event | category | flops | bytes accessed | tf_op | source)
XLA Modules:
  0.0 134.7 jit_solution(9929929804944049070)
XLA Ops:
  7.2 1.0 convert_element_type.9
  8.2 0.9 copy-done.1
  9.2 3.4 %collective-permute-start = (f32[12,1,512]{2,1,0:T(1,128)S(1)}, f32[12,1,512]{2,1,0:T(1,128)S(1)}, u32[]{:S(2)}, u32[]{:S(2)}) collective-permute-start(f32[12,1,512]{2,1,0:T(1,128)S(1)} %get-tuple-element.54), channel_id=1, source_target_pairs={{0,8},{8,16},{16,24},{24,32},{32,40},{40,48},{48,56},{56,64},{64,7... | collective-permute-start | bytes 73736 | tf_op jit(solution)/shard_map/ppermute | solution.py:14
  12.6 1.3 collective-permute-start.1
  13.9 0.2 collective-permute-done
  14.1 0.1 add_add_fusion
  14.2 4.1 %collective-permute-done.1 = f32[12,1,512]{2,1,0:T(1,128)S(1)} collective-permute-done((f32[12,1,512]{2,1,0:T(1,128)S(1)}, f32[12,1,512]{2,1,0:T(1,128)S(1)}, u32[]{:S(2)}, u32[]{:S(2)}) %collective-permute-start.1) | collective-permute-done | bytes 24608 | tf_op jit(solution)/shard_map/ppermute | solution.py:15
  18.3 0.2 pad_maximum_fusion.19
  18.5 1.9 %collective-permute-start.3 = (f32[12,34,1]{2,1,0:T(8,128)S(1)}, f32[12,34,1]{2,1,0:T(8,128)S(1)}, u32[]{:S(2)}, u32[]{:S(2)}) collective-permute-start(f32[12,34,1]{2,1,0:T(8,128)S(1)} %get-tuple-element.39), channel_id=1, source_target_pairs={{0,1},{1,2},{2,3},{3,4},{4,5},{5,6},{6,7},{8,9},{9,10},{10,11},{11... | collective-permute-start | bytes 4904 | tf_op jit(solution)/shard_map/ppermute | solution.py:14
  20.4 3.6 %collective-permute-start.2 = (f32[12,34,1]{2,1,0:T(8,128)S(1)}, f32[12,34,1]{2,1,0:T(8,128)S(1)}, u32[]{:S(2)}, u32[]{:S(2)}) collective-permute-start(f32[12,34,1]{2,1,0:T(8,128)S(1)} %get-tuple-element.38), channel_id=1, source_target_pairs={{1,0},{2,1},{3,2},{4,3},{5,4},{6,5},{7,6},{9,8},{10,9},{11,10},{12... | collective-permute-start | bytes 4904 | tf_op jit(solution)/shard_map/ppermute | solution.py:15
  24.1 0.1 slice_select_fusion
  24.3 0.2 pad_multiply_fusion.14
  24.6 0.1 fusion.1
  24.9 0.1 pad_multiply_fusion.13
  25.0 0.1 multiply_add_fusion.11
  25.4 0.1 pad_multiply_fusion.11
  25.5 0.1 multiply_add_fusion.10
  25.9 0.1 multiply_add_fusion.9
  26.1 0.1 multiply_add_fusion.8
  26.2 0.5 copy-done.6
  26.8 0.9 collective-permute-done.2
  27.8 0.8 fusion.6
  28.7 0.1 fusion.30
  28.8 0.4 multiply_add_fusion.3
  29.2 0.1 fusion.29
  29.3 0.4 multiply_add_fusion.2
  29.7 0.2 fusion.28
  29.9 0.3 multiply_add_fusion.1
  30.2 0.1 fusion.27
  30.4 0.3 multiply_add_fusion
  30.7 0.3 add_divide_fusion
  31.2 1.5 %collective-permute-start.4 = (f32[3,4,512]{2,0,1:T(4,128)S(1)}, f32[3,4,512]{2,0,1:T(4,128)S(1)}, u32[]{:S(2)}, u32[]{:S(2)}) collective-permute-start(f32[3,4,512]{2,0,1:T(4,128)S(1)} %pad_maximum_fusion.20), channel_id=1, source_target_pairs={{8,0},{16,8},{24,16},{32,24},{40,32},{48,40},{56,48},{64,56},{72,6... | collective-permute-start | bytes 73736 | tf_op jit(solution)/shard_map/ppermute | solution.py:23
  32.7 4.3 %collective-permute-done.4 = f32[3,4,512]{2,0,1:T(4,128)S(1)} collective-permute-done((f32[3,4,512]{2,0,1:T(4,128)S(1)}, f32[3,4,512]{2,0,1:T(4,128)S(1)}, u32[]{:S(2)}, u32[]{:S(2)}) %collective-permute-start.4) | collective-permute-done | bytes 24608 | tf_op jit(solution)/shard_map/ppermute | solution.py:23
  37.1 0.7 pad_maximum_fusion.21
  37.8 79.5 %all-gather.3.cloned.1.call-done = f32[4,4,16384]{2,0,1:T(4,128)} async-done(((f32[4,4,512]{2,0,1:T(4,128)}), f32[4,4,16384]{2,0,1:T(4,128)}) %all-gather.3.cloned.1.call-update) | async-done | bytes 1048592 | tf_op jit(solution)/shard_map/all_gather | solution.py:116
  117.2 1.9 %reshape.107 = f32[4,4,32,512]{3,2,0,1:T(8,128)S(1)} reshape(f32[4,4,16384]{2,0,1:T(4,128)} %all-gather.3.cloned.1.call-done) | data formatting | bytes 2097152 | tf_op jit(solution)/shard_map/all_gather | solution.py:116
  119.3 1.2 copy-done
  120.4 3.0 %slice_reduce_fusion = (f32[4,16384]{1,0:T(4,128)S(1)}, f32[4,16384]{1,0:T(4,128)S(1)}, f32[4,16384]{1,0:T(4,128)S(1)}, f32[4,16384]{1,0:T(4,128)S(1)}) fusion(f32[4,4,16384]{2,0,1:T(4,128)S(1)} %copy-done), kind=kLoop, calls=%fused_computation.14 | loop fusion | bytes 2097152 | tf_op jit(solution)/shard_map/slice | solution.py:117
  123.6 0.3 copy_bitcast_fusion
  124.1 0.3 multiply_add_fusion.7
  124.5 0.4 fusion.19
  125.0 0.2 multiply_add_fusion.6
  125.3 0.4 fusion.17
  125.8 0.2 multiply_add_fusion.5
  126.0 0.3 fusion.15
  126.4 0.2 pad_multiply_fusion
  126.8 0.2 fusion.12
  127.1 0.7 pad_maximum_fusion.14
  (73 shorter events, 2.3 us)
Async XLA Ops:
  7.2 1.0 copy-start.3
  7.2 110.1 %all-gather.3.cloned.1.call-start = ((), (), s32[]{:S(2)}) async-start(), calls=%async_computation | async-start | bytes 1081344 | tf_op jit(solution)/shard_map/all_gather | solution.py:116
  8.2 1.0 copy-start.1
  9.2 4.9 %collective-permute-start = (f32[12,1,512]{2,1,0:T(1,128)S(1)}, f32[12,1,512]{2,1,0:T(1,128)S(1)}, u32[]{:S(2)}, u32[]{:S(2)}) collective-permute-start(f32[12,1,512]{2,1,0:T(1,128)S(1)} %get-tuple-element.54), channel_id=1, source_target_pairs={{0,8},{8,16},{16,24},{24,32},{32,40},{40,48},{48,56},{56,64},{64,7... | collective-permute-start | bytes 73736 | tf_op jit(solution)/shard_map/ppermute | solution.py:14
  12.6 5.7 %collective-permute-start.1 = (f32[12,1,512]{2,1,0:T(1,128)S(1)}, f32[12,1,512]{2,1,0:T(1,128)S(1)}, u32[]{:S(2)}, u32[]{:S(2)}) collective-permute-start(f32[12,1,512]{2,1,0:T(1,128)S(1)} %get-tuple-element.53), channel_id=1, source_target_pairs={{8,0},{16,8},{24,16},{32,24},{40,32},{48,40},{56,48},{64,56},{72,6... | collective-permute-start | bytes 73736 | tf_op jit(solution)/shard_map/ppermute | solution.py:15
  18.5 5.6 %copy-start.5 = (pred[31]{0:T(512)(128)(4,1)S(1)}, pred[31]{0:T(512)(128)(4,1)}, u32[]{:S(2)}) copy-start(pred[31]{0:T(512)(128)(4,1)} %constant.15.clone.1) | copy-start | bytes 97
  18.5 8.3 %collective-permute-start.3 = (f32[12,34,1]{2,1,0:T(8,128)S(1)}, f32[12,34,1]{2,1,0:T(8,128)S(1)}, u32[]{:S(2)}, u32[]{:S(2)}) collective-permute-start(f32[12,34,1]{2,1,0:T(8,128)S(1)} %get-tuple-element.39), channel_id=1, source_target_pairs={{0,1},{1,2},{2,3},{3,4},{4,5},{5,6},{6,7},{8,9},{9,10},{10,11},{11... | collective-permute-start | bytes 4904 | tf_op jit(solution)/shard_map/ppermute | solution.py:14
  20.4 7.3 %collective-permute-start.2 = (f32[12,34,1]{2,1,0:T(8,128)S(1)}, f32[12,34,1]{2,1,0:T(8,128)S(1)}, u32[]{:S(2)}, u32[]{:S(2)}) collective-permute-start(f32[12,34,1]{2,1,0:T(8,128)S(1)} %get-tuple-element.38), channel_id=1, source_target_pairs={{1,0},{2,1},{3,2},{4,3},{5,4},{6,5},{7,6},{9,8},{10,9},{11,10},{12... | collective-permute-start | bytes 4904 | tf_op jit(solution)/shard_map/ppermute | solution.py:15
  26.1 0.7 copy-start.6
  26.7 1.0 copy-start.4
  28.5 8.5 %copy-start.2 = (f32[4,32,512]{2,1,0:T(8,128)}, f32[4,32,512]{2,1,0:T(8,128)S(1)}, u32[]{:S(2)}) copy-start(f32[4,32,512]{2,1,0:T(8,128)S(1)} %fusion.6) | copy-start | bytes 786436
  31.2 5.8 %collective-permute-start.4 = (f32[3,4,512]{2,0,1:T(4,128)S(1)}, f32[3,4,512]{2,0,1:T(4,128)S(1)}, u32[]{:S(2)}, u32[]{:S(2)}) collective-permute-start(f32[3,4,512]{2,0,1:T(4,128)S(1)} %pad_maximum_fusion.20), channel_id=1, source_target_pairs={{8,0},{16,8},{24,16},{32,24},{40,32},{48,40},{56,48},{64,56},{72,6... | collective-permute-start | bytes 73736 | tf_op jit(solution)/shard_map/ppermute | solution.py:23
  119.2 1.2 copy-start
Sparse Core Ops, SparseCore 0:
  37.9 79.3 all-gather.2
where the time goes:
time: 135 us
  waiting for transfers between devices  89 us (66%)
  between operations  14.8 us (11%)
  starting transfers between devices  11.8 us (9%)
  local copies, waits for them, and re-layouts  9.68 us (7%)
  other arithmetic  9.43 us (7%)
    all_gather x1, waiting for transfers between devices, shards(): gathered = lax.all_gather(system, 'gx', axis=2, tiled=True)  79.5 us
    ppermute x2, starting transfers between devices, extended(): before = lax.ppermute(last, axis, up)  5.32 us
    ppermute x2, waiting for transfers between devices, extended(): after = lax.ppermute(leading, axis, down)  5 us
    ppermute x2, starting transfers between devices, extended(): after = lax.ppermute(leading, axis, down)  4.93 us
    ppermute x1, waiting for transfers between devices, passed_along(): lax.ppermute(value, axis, [(source, source + steps) for source in range(l...  4.33 us
    slice x1, local copies, waits for them, and re-layouts, shards(): gathered[2]  3.03 us
    unnamed x18, local copies, waits for them, and re-layouts  2.75 us
  transfers between devices with their start and end apart: 6, of which 5 were waited for; matrix products, arithmetic and copies ran while one was open for 2% of the time, Pallas kernels for 0%

commit v1 on v0

v1 whole, which is shorter than its diff:
```python
import jax
import jax.numpy as jnp
from jax import lax
from jax.experimental import pallas as pl
from jax.experimental.pallas import tpu as pltpu
from jax.sharding import PartitionSpec as P

MESH = pl.DeviceIdType.MESH
PL = 4
R = 32
W = 512
NB = 32
NS = 4
NV = 6


def sweep_kernel(u_ref, kx_ref, ky_ref, g_ref, o_ref, r_ref,
                 rows_s, cols_s, hrow, hcol, hcor,
                 ik_s, r_s, a_s, b_s, v_s, msg, inbox, res, xf,
                 hs, hr, ms, mr, rs, rr):
    me = lax.axis_index("gx")
    gy = lax.axis_index("gy")
    prev, nxt = lax.rem(me + NB - 1, NB), lax.rem(me + 1, NB)
    west, east = lax.rem(gy + 7, 8), lax.rem(gy + 1, 8)

    def signal(dev):
        pl.semaphore_signal(barrier, inc=1, device_id=dev, device_id_type=MESH)

    barrier = pltpu.get_barrier_semaphore()
    is_solver = me < NS

    @pl.when(is_solver)
    def _():
        for k in range(1, NB):
            signal((lax.rem(me + k, NB), gy))

    for dev in ((prev, gy), (nxt, gy), (me, west), (me, east),
                (prev, west), (prev, east), (nxt, west), (nxt, east)):
        signal(dev)

    lane = lax.broadcasted_iota(jnp.int32, (8, 128), 1)
    for p in range(PL):
        rows_s[0, p:p + 1, :] = u_ref[R * p:R * p + 1, :]
        rows_s[1, p:p + 1, :] = u_ref[R * p + R - 1:R * p + R, :]
    kyf = ky_ref[...].astype(jnp.float32)
    to_east = jnp.zeros((8, 128), jnp.float32)
    to_west = jnp.zeros((8, 128), jnp.float32)
    for m in range(16):
        sl = slice(8 * m, 8 * m + 8)
        to_east = jnp.where(lane == m, pltpu.roll(u_ref[sl, 384:512], (m + 1) % 128, 1), to_east)
        to_east = jnp.where(lane == 16 + m, pltpu.roll(kyf[sl, 384:512], (m + 17) % 128, 1), to_east)
        to_west = jnp.where(lane == m, pltpu.roll(u_ref[sl, 0:128], m, 1) if m else u_ref[sl, 0:128], to_west)
    cols_s[0] = to_east
    cols_s[1] = to_west

    pl.semaphore_wait(barrier, 8 + NS - is_solver.astype(jnp.int32))

    def send(src, dst, i, dev):
        c = pltpu.make_async_remote_copy(src_ref=src, dst_ref=dst, send_sem=hs.at[i], recv_sem=hr.at[i],
                                         device_id=dev, device_id_type=MESH)
        c.start()
        return c

    halos = [
        send(rows_s.at[1], hrow.at[0], 0, (nxt, gy)),
        send(rows_s.at[0], hrow.at[1], 1, (prev, gy)),
        send(cols_s.at[0], hcol.at[0], 2, (me, east)),
        send(cols_s.at[1], hcol.at[1], 3, (me, west)),
        send(rows_s.at[1, :, pl.ds(384, 128)], hcor.at[0], 4, (nxt, east)),
        send(rows_s.at[1, :, pl.ds(0, 128)], hcor.at[1], 5, (nxt, west)),
        send(rows_s.at[0, :, pl.ds(384, 128)], hcor.at[2], 6, (prev, east)),
        send(rows_s.at[0, :, pl.ds(0, 128)], hcor.at[3], 7, (prev, west)),
    ]

    ik = 1.0 / kx_ref[...].astype(jnp.float32)
    for q in range(NS):
        ik_s[128 * q:128 * q + 128, :] = ik[:, 128 * q:128 * q + 128]
    a = d = jnp.ones((16, 128), jnp.float32)
    b = c = jnp.zeros((16, 128), jnp.float32)
    for i in range(R):
        row = pl.ds(i, 16, stride=R)
        a_s[row, :] = a
        b_s[row, :] = b
        ik = ik_s[row, :]
        c = c + a
        a = a + c * ik
        d = d + b
        b = b + d * ik

    def put(k, value):
        for q in range(NS):
            msg[q, 4 * k:4 * k + 4, :] = value[4 * q:4 * q + 4, :]

    for k, value in enumerate((a, b, c, d)):
        put(k, value)

    for h in halos:
        h.wait()

    lane_w = lax.broadcasted_iota(jnp.int32, (R, W), 1)
    row_w = lax.broadcasted_iota(jnp.int32, (R, W), 0)
    lane_p = lax.broadcasted_iota(jnp.int32, (PL, W), 1)
    col_w = jnp.where(gy == 0, 0.0, hcol[0])
    col_e = jnp.where(gy == 7, 0.0, hcol[1])

    def wide(tile, at_end):
        rest = jnp.zeros((tile.shape[0], W - 128), jnp.float32)
        return jnp.concatenate([rest, tile] if at_end else [tile, rest], axis=1)

    def halo_diff(row, cor_w, cor_e, missing):
        cw = jnp.where(gy == 0, 0.0, cor_w)
        ce = jnp.where(gy == 7, 0.0, cor_e)
        w = jnp.where(lane_p == 0, wide(pltpu.roll(cw, 1, 1), False), pltpu.roll(row, 1, 1))
        e = jnp.where(lane_p == W - 1, wide(pltpu.roll(ce, 127, 1), True), pltpu.roll(row, W - 1, 1))
        return jnp.where(missing, 0.0, e - w)

    d_prev = halo_diff(hrow[0], hcor[0], hcor[1], me == 0)
    d_next = halo_diff(hrow[1], hcor[2], hcor[3], me == NB - 1)

    for p in range(PL):
        sl = slice(R * p, R * p + R)
        u = u_ref[sl, :]
        ky = ky_ref[sl, :].astype(jnp.float32)
        g = g_ref[sl, :].astype(jnp.float32)
        cw, ck, ce = [], [], []
        for q in range(4):
            m = 4 * p + q
            cw.append(pltpu.roll(col_w, 128 - m, 1) if m else col_w)
            ck.append(pltpu.roll(col_w, 112 - m, 1))
            ce.append(pltpu.roll(col_e, 127 - m, 1))
        cw, ck, ce = (jnp.concatenate(t, axis=0) for t in (cw, ck, ce))
        uw = jnp.where(lane_w == 0, wide(cw, False), pltpu.roll(u, 1, 1))
        kb = jnp.where(lane_w == 0, wide(ck, False), pltpu.roll(ky, 1, 1))
        ue = jnp.where(lane_w == W - 1, wide(ce, True), pltpu.roll(u, W - 1, 1))
        dd = ue - uw
        up = jnp.where(row_w == 0, d_prev[p:p + 1, :], pltpu.roll(dd, 1, 0))
        dn = jnp.where(row_w == R - 1, d_next[p:p + 1, :], pltpu.roll(dd, R - 1, 0))
        right = u + (ky * (ue - u) - kb * (u - uw)) + g * (dn - up) * 0.25
        r_ref[sl, :] = right
        for q in range(NS):
            r_s[128 * q + R * p:128 * q + R * p + R, :] = right[:, 128 * q:128 * q + 128]

    vx = vf = jnp.zeros((16, 128), jnp.float32)
    for i in range(R):
        row = pl.ds(i, 16, stride=R)
        v_s[row, :] = vx
        vf = vf + (vx - r_s[row, :])
        vx = vx + vf * ik_s[row, :]
    put(4, vx)
    put(5, vf)

    def map_copy(s):
        return pltpu.make_async_remote_copy(
            src_ref=msg.at[s],
            dst_ref=inbox.at[me],
            send_sem=ms.at[s], recv_sem=mr, device_id=(s, gy), device_id_type=MESH)

    for s in range(NS):
        @pl.when(me != s)
        def _():
            map_copy(s).start()

    @pl.when(is_solver)
    def _():
        for s in range(NS):
            @pl.when(me == s)
            def _():
                inbox[s] = msg[s]
        part = inbox.at[pl.ds(0, NB - 1)]
        pltpu.make_async_copy(part, part, mr).wait()

        def block(p):
            return [inbox[p, 4 * k:4 * k + 4, :] for k in range(NV)]

        groups = []
        for z in range(8):
            a, b, c, d, vx, vf = block(4 * z)
            for x in range(1, 4):
                a2, b2, c2, d2, vx2, vf2 = block(4 * z + x)
                a, c = a2 * a + b2 * c, c2 * a + d2 * c
                b, d = a2 * b + b2 * d, c2 * b + d2 * d
                vx, vf = a2 * vx + b2 * vf + vx2, c2 * vx + d2 * vf + vf2
            groups.append((a, b, c, d, vx, vf))
        zero = jnp.zeros((PL, 128), jnp.float32)
        left = [(zero, zero)]
        for z in range(7):
            a, b, c, d, vx, vf = groups[z]
            gl, jl = left[-1]
            inv = 1.0 / (a + b * gl)
            gn = (c + d * gl) * inv
            left.append((gn, jl * inv + vf - gn * vx))
        a, b, c, d, vx, vf = groups[7]
        inv = 1.0 / b
        right = [(a * inv, -vx * inv)]
        for z in range(6, -1, -1):
            a, b, c, d, vx, vf = groups[z]
            gr, jr = right[0]
            inv = 1.0 / (d + gr * b)
            right.insert(0, ((c + gr * a) * inv, (jr - vf - gr * vx) * inv))
        for z in range(8):
            gl, jl = left[z]
            gr, jr = right[z]
            x0 = (jr - jl) / (gl + gr)
            f0 = gl * x0 + jl
            for x in range(4):
                p = 4 * z + x
                res[p, 0:4, :] = x0
                res[p, 4:8, :] = f0
                if x < 3:
                    a, b, c, d, vx, vf = block(p)
                    x0, f0 = a * x0 + b * f0 + vx, c * x0 + d * f0 + vf

        for k in range(1, NB):
            p = lax.rem(me + k, NB)
            pltpu.make_async_remote_copy(
                src_ref=res.at[p], dst_ref=xf.at[me],
                send_sem=rs, recv_sem=rr.at[me], device_id=(p, gy), device_id_type=MESH).start()
        for s in range(NS):
            @pl.when(me == s)
            def _():
                xf[s] = res[s]

    for s in range(NS):
        @pl.when(me != s)
        def _():
            pltpu.make_async_copy(xf.at[s], xf.at[s], rr.at[s]).wait()

    for s in range(NS):
        ls = slice(128 * s, 128 * s + 128)
        for p in range(PL):
            sl = slice(R * p, R * p + R)
            x0 = xf[s, p:p + 1, :]
            f0 = xf[s, 4 + p:5 + p, :]
            ts = slice(128 * s + R * p, 128 * s + R * p + R)
            o_ref[sl, ls] = a_s[ts, :] * x0 + b_s[ts, :] * f0 + v_s[ts, :]

    for s in range(NS):
        @pl.when(me != s)
        def _():
            map_copy(s).wait_send()

    @pl.when(is_solver)
    def _():
        part = res.at[pl.ds(0, NB - 1)]
        pltpu.make_async_copy(part, part, rs).wait()


def shards(state_field, x_coupling, y_coupling, cross_coeff):
    flat = (PL * R, W)
    vmem = pl.BlockSpec(memory_space=pltpu.VMEM)
    f32 = jnp.float32
    big = pltpu.VMEM((NS * PL * R, 128), f32)
    dma = pltpu.SemaphoreType.DMA
    out, rhs = pl.pallas_call(
        sweep_kernel,
        out_shape=(jax.ShapeDtypeStruct(flat, f32),) * 2,
        in_specs=[vmem] * 4,
        out_specs=(vmem, vmem),
        scratch_shapes=[
            pltpu.VMEM((2, PL, W), f32), pltpu.VMEM((2, 8, 128), f32),
            pltpu.VMEM((2, PL, W), f32), pltpu.VMEM((2, 8, 128), f32), pltpu.VMEM((4, PL, 128), f32),
            big, big, big, big, big,
            pltpu.VMEM((NS, PL * NV, 128), f32), pltpu.VMEM((NB, PL * NV, 128), f32),
            pltpu.VMEM((NB, 8, 128), f32), pltpu.VMEM((NS, 8, 128), f32),
            dma((8,)), dma((8,)), dma((NS,)), dma(()), dma(()), dma((NS,)),
        ],
        compiler_params=pltpu.CompilerParams(
            collective_id=0, has_side_effects=True, vmem_limit_bytes=32 * 2**20),
    )(state_field.reshape(flat), x_coupling.reshape(flat), y_coupling.reshape(flat), cross_coeff.reshape(flat))
    return out.reshape(state_field.shape), rhs.reshape(state_field.shape)


def solution(mesh):
    spec = P(None, "gx", "gy")
    return jax.shard_map(shards, mesh=mesh, in_specs=(spec,) * 4, out_specs=(spec, spec), check_vma=False)
```

time: 135 us -> 31.6 us (0.23)
  the two profiles are of different devices: /device:TPU:8 before, /device:TPU:1 now
where the time goes in v1:
time: 31.6 us; the launch traced here: 31.5 us
  Pallas kernels  25.8 us (82%)
  local copies, waits for them, and re-layouts  5.06 us (16%)
  between operations  0.65 us (2%)
    pallas_call x1, Pallas kernels, shards(): pl.pallas_call(sweep_kernel, out_shape=(jax.ShapeDtypeStruct(flat, f32),)...  25.8 us
    unnamed x10, local copies, waits for them, and re-layouts  5.06 us

profile of v1, /device:TPU:1, one launch (start us, length us, event | category | flops | bytes accessed | tf_op | source)
XLA Modules:
  0.0 31.5 jit_solution(16113176107595707870)
XLA Ops:
  0.6 0.0 copy-start
  0.6 0.9 %copy-done = f32[4,32,512]{2,1,0:T(8,128)S(1)} copy-done((f32[4,32,512]{2,1,0:T(8,128)S(1)}, f32[4,32,512]{2,1,0:T(8,128)}, u32[]{:S(2)}) %copy-start) | copy-done | bytes 262168
  1.6 0.0 copy-start.1
  1.6 0.9 %copy-done.1 = bf16[4,32,512]{2,1,0:T(8,128)(2,1)S(1)} copy-done((bf16[4,32,512]{2,1,0:T(8,128)(2,1)S(1)}, bf16[4,32,512]{2,1,0:T(8,128)(2,1)}, u32[]{:S(2)}) %copy-start.1) | copy-done | bytes 131096
  2.5 0.0 copy-start.2
  2.5 0.9 %copy-done.2 = bf16[4,32,512]{2,1,0:T(8,128)(2,1)S(1)} copy-done((bf16[4,32,512]{2,1,0:T(8,128)(2,1)S(1)}, bf16[4,32,512]{2,1,0:T(8,128)(2,1)}, u32[]{:S(2)}) %copy-start.2) | copy-done | bytes 131096
  3.4 0.0 copy-start.3
  3.4 0.9 %copy-done.3 = bf16[4,32,512]{2,1,0:T(8,128)(2,1)S(1)} copy-done((bf16[4,32,512]{2,1,0:T(8,128)(2,1)S(1)}, bf16[4,32,512]{2,1,0:T(8,128)(2,1)}, u32[]{:S(2)}) %copy-start.3) | copy-done | bytes 131096
  4.3 25.8 %shard_map.59 = (f32[128,512]{1,0:T(8,128)S(1)}, f32[128,512]{1,0:T(8,128)S(1)}) custom-call(f32[128,512]{1,0:T(8,128)S(1)} %bitcast.6, bf16[128,512]{1,0:T(8,128)(2,1)S(1)} %bitcast.9, bf16[128,512]{1,0:T(8,128)(2,1)S(1)} %bitcast.10, bf16[128,512]{1,0:T(8,128)(2,1)S(1)} %bitcast.11), custom_call_target="tpu_custom_call" | custom-call | tf_op jit(solution)/shard_map/pallas_call | solution.py:254
  30.1 0.7 %copy.8 = f32[4,32,512]{2,1,0:T(8,128)} copy(f32[4,32,512]{2,1,0:T(8,128)S(1)} %bitcast.8) | data formatting | bytes 524288
  30.8 0.7 %copy.9 = f32[4,32,512]{2,1,0:T(8,128)} copy(f32[4,32,512]{2,1,0:T(8,128)S(1)} %bitcast.7) | data formatting | bytes 524288
Async XLA Ops:
  0.6 1.0 %copy-start = (f32[4,32,512]{2,1,0:T(8,128)S(1)}, f32[4,32,512]{2,1,0:T(8,128)}, u32[]{:S(2)}) copy-start(f32[4,32,512]{2,1,0:T(8,128)} %param.4) | copy-start | bytes 786436
  1.6 0.9 %copy-start.1 = (bf16[4,32,512]{2,1,0:T(8,128)(2,1)S(1)}, bf16[4,32,512]{2,1,0:T(8,128)(2,1)}, u32[]{:S(2)}) copy-start(bf16[4,32,512]{2,1,0:T(8,128)(2,1)} %param.5) | copy-start | bytes 393220
  2.5 0.9 %copy-start.2 = (bf16[4,32,512]{2,1,0:T(8,128)(2,1)S(1)}, bf16[4,32,512]{2,1,0:T(8,128)(2,1)}, u32[]{:S(2)}) copy-start(bf16[4,32,512]{2,1,0:T(8,128)(2,1)} %param.6) | copy-start | bytes 393220
  3.4 0.9 %copy-start.3 = (bf16[4,32,512]{2,1,0:T(8,128)(2,1)S(1)}, bf16[4,32,512]{2,1,0:T(8,128)(2,1)}, u32[]{:S(2)}) copy-start(bf16[4,32,512]{2,1,0:T(8,128)(2,1)} %param.7) | copy-start | bytes 393220

commit v2 on v1

--- a/solution.py
+++ b/solution.py
@@ -14,10 +14,15 @@
 NV = 6
 
 
-def sweep_kernel(u_ref, kx_ref, ky_ref, g_ref, o_ref, r_ref,
+def sweep_kernel(u_hbm, kx_hbm, ky_hbm, g_hbm, r_ref, a_s, b_s, v_s, xf,
+                 u_ref, kx_ref, ky_ref, g_ref,
                  rows_s, cols_s, hrow, hcol, hcor,
-                 ik_s, r_s, a_s, b_s, v_s, msg, inbox, res, xf,
-                 hs, hr, ms, mr, rs, rr):
+                 ik_s, r_s, msg, inbox, res,
+                 ls, hs, hr, ms, mr, rs, rr):
+    loads = [pltpu.make_async_copy(src, dst, ls.at[i]) for i, (src, dst) in enumerate(
+        ((u_hbm, u_ref), (ky_hbm, ky_ref), (kx_hbm, kx_ref), (g_hbm, g_ref)))]
+    for load in loads:
+        load.start()
     me = lax.axis_index("gx")
     gy = lax.axis_index("gy")
     prev, nxt = lax.rem(me + NB - 1, NB), lax.rem(me + 1, NB)
@@ -37,6 +42,9 @@
     for dev in ((prev, gy), (nxt, gy), (me, west), (me, east),
                 (prev, west), (prev, east), (nxt, west), (nxt, east)):
         signal(dev)
+
+    loads[0].wait()
+    loads[1].wait()
 
     lane = lax.broadcasted_iota(jnp.int32, (8, 128), 1)
     for p in range(PL):
@@ -72,6 +80,7 @@
         send(rows_s.at[0, :, pl.ds(0, 128)], hcor.at[3], 7, (prev, west)),
     ]
 
+    loads[2].wait()
     ik = 1.0 / kx_ref[...].astype(jnp.float32)
     for q in range(NS):
         ik_s[128 * q:128 * q + 128, :] = ik[:, 128 * q:128 * q + 128]
@@ -94,6 +103,7 @@
     for k, value in enumerate((a, b, c, d)):
         put(k, value)
 
+    loads[3].wait()
     for h in halos:
         h.wait()
 
@@ -211,7 +221,7 @@
                     x0, f0 = a * x0 + b * f0 + vx, c * x0 + d * f0 + vf
 
         for k in range(1, NB):
-            p = lax.rem(me + k, NB)
+            p = lax.rem(me + k, NS) if k < NS else k
             pltpu.make_async_remote_copy(
                 src_ref=res.at[p], dst_ref=xf.at[me],
                 send_sem=rs, recv_sem=rr.at[me], device_id=(p, gy), device_id_type=MESH).start()
@@ -226,15 +236,6 @@
             pltpu.make_async_copy(xf.at[s], xf.at[s], rr.at[s]).wait()
 
     for s in range(NS):
-        ls = slice(128 * s, 128 * s + 128)
-        for p in range(PL):
-            sl = slice(R * p, R * p + R)
-            x0 = xf[s, p:p + 1, :]
-            f0 = xf[s, 4 + p:5 + p, :]
-            ts = slice(128 * s + R * p, 128 * s + R * p + R)
-            o_ref[sl, ls] = a_s[ts, :] * x0 + b_s[ts, :] * f0 + v_s[ts, :]
-
-    for s in range(NS):
         @pl.when(me != s)
         def _():
             map_copy(s).wait_send()
@@ -245,28 +246,62 @@
         pltpu.make_async_copy(part, part, rs).wait()
 
 
+def finish_kernel(r_ref, a_ref, b_ref, v_ref, xf_ref, o_hbm, r_hbm, o_ref, sems):
+    right = pltpu.make_async_copy(r_ref, r_hbm, sems.at[PL])
+    right.start()
+    copies = []
+    for p in range(PL):
+        sl = slice(R * p, R * p + R)
+        for s in range(NS):
+            x0 = xf_ref[s, p:p + 1, :]
+            f0 = xf_ref[s, 4 + p:5 + p, :]
+            ts = slice(128 * s + R * p, 128 * s + R * p + R)
+            o_ref[sl, 128 * s:128 * s + 128] = a_ref[ts, :] * x0 + b_ref[ts, :] * f0 + v_ref[ts, :]
+        part = pl.ds(R * p, R)
+        copies.append(pltpu.make_async_copy(o_ref.at[part], o_hbm.at[part], sems.at[p]))
+        copies[-1].start()
+    for copy in copies:
+        copy.wait()
+    right.wait()
+
+
 def shards(state_field, x_coupling, y_coupling, cross_coeff):
     flat = (PL * R, W)
     vmem = pl.BlockSpec(memory_space=pltpu.VMEM)
-    f32 = jnp.float32
-    big = pltpu.VMEM((NS * PL * R, 128), f32)
+    hbm = pl.BlockSpec(memory_space=pltpu.HBM)
+    f32, bf16 = jnp.float32, jnp.bfloat16
+    tiles = (NS * PL * R, 128)
+    big = pltpu.VMEM(tiles, f32)
     dma = pltpu.SemaphoreType.DMA
-    out, rhs = pl.pallas_call(
+    shape = jax.ShapeDtypeStruct
+    args = [pltpu.with_memory_space_constraint(x.reshape(flat), pltpu.HBM)
+            for x in (state_field, x_coupling, y_coupling, cross_coeff)]
+    parts = pl.pallas_call(
         sweep_kernel,
-        out_shape=(jax.ShapeDtypeStruct(flat, f32),) * 2,
-        in_specs=[vmem] * 4,
-        out_specs=(vmem, vmem),
+        out_shape=(shape(flat, f32), shape(tiles, f32), shape(tiles, f32), shape(tiles, f32),
+                   shape((NS, 8, 128), f32)),
+        in_specs=[hbm] * 4,
+        out_specs=(vmem,) * 5,
         scratch_shapes=[
+            pltpu.VMEM(flat, f32), pltpu.VMEM(flat, bf16), pltpu.VMEM(flat, bf16), pltpu.VMEM(flat, bf16),
             pltpu.VMEM((2, PL, W), f32), pltpu.VMEM((2, 8, 128), f32),
             pltpu.VMEM((2, PL, W), f32), pltpu.VMEM((2, 8, 128), f32), pltpu.VMEM((4, PL, 128), f32),
-            big, big, big, big, big,
+            big, big,
             pltpu.VMEM((NS, PL * NV, 128), f32), pltpu.VMEM((NB, PL * NV, 128), f32),
-            pltpu.VMEM((NB, 8, 128), f32), pltpu.VMEM((NS, 8, 128), f32),
-            dma((8,)), dma((8,)), dma((NS,)), dma(()), dma(()), dma((NS,)),
+            pltpu.VMEM((NB, 8, 128), f32),
+            dma((4,)), dma((8,)), dma((8,)), dma((NS,)), dma(()), dma(()), dma((NS,)),
         ],
         compiler_params=pltpu.CompilerParams(
             collective_id=0, has_side_effects=True, vmem_limit_bytes=32 * 2**20),
-    )(state_field.reshape(flat), x_coupling.reshape(flat), y_coupling.reshape(flat), cross_coeff.reshape(flat))
+    )(*args)
+    out, rhs = pl.pallas_call(
+        finish_kernel,
+        out_shape=(shape(flat, f32),) * 2,
+        in_specs=[vmem] * 5,
+        out_specs=(hbm, hbm),
+        scratch_shapes=[pltpu.VMEM(flat, f32), dma((PL + 1,))],
+        compiler_params=pltpu.CompilerParams(vmem_limit_bytes=32 * 2**20),
+    )(*parts)
     return out.reshape(state_field.shape), rhs.reshape(state_field.shape)
 
 

time: 31.6 us -> 27.3 us (0.86)
  local copies, waits for them, and re-layouts: 5.06 us -> 0 us
  Pallas kernels: 25.8 us -> 26.6 us
    unnamed x10 -> x0, local copies, waits for them, and re-layouts: 5.06 us -> none
    pallas_call x1 -> x2, Pallas kernels: 25.8 us -> 26.6 us  [the longest x1 25.8 us: shards(): pl.pallas_call(sweep_kernel, out_shape=(shape(flat, f32), shape(tiles, f3...]
where the time goes in v2:
time: 27.3 us; the launch traced here: 27.2 us
  Pallas kernels  26.6 us (97%)
  between operations  0.64 us (2%)
    pallas_call x1, Pallas kernels, shards(): pl.pallas_call(sweep_kernel, out_shape=(shape(flat, f32), shape(tiles, f3...  25.8 us
    pallas_call x1, Pallas kernels, shards(): pl.pallas_call(finish_kernel, out_shape=(shape(flat, f32),) * 2, in_specs...  0.83 us

profile of v2, /device:TPU:1, one launch (start us, length us, event | category | flops | bytes accessed | tf_op | source)
XLA Modules:
  0.0 27.2 jit_solution(4672552870023571861)
XLA Ops:
  0.6 25.8 %shard_map.59 = (f32[128,512]{1,0:T(8,128)S(1)}, f32[512,128]{1,0:T(8,128)S(1)}, f32[512,128]{1,0:T(8,128)S(1)}, f32[512,128]{1,0:T(8,128)S(1)}, f32[4,8,128]{2,1,0:T(8,128)S(1)}) custom-call(f32[128,512]{1,0:T(8,128)} %bitcast.6, bf16[128,512]{1,0:T(8,128)(2,1)} %bitcast.7, bf16[128,512]{1,0:T(8,128)(2,1)} %bitcast.8, bf16[128,512]{1,0:T(8,128)(2,1)} %bitcast.9), custom_call_target="tpu_custom_call" | custom-call | tf_op jit(solution)/shard_map/pallas_call | solution.py:279
  26.4 0.8 %shard_map.60 = (f32[128,512]{1,0:T(8,128)}, f32[128,512]{1,0:T(8,128)}) custom-call(f32[128,512]{1,0:T(8,128)S(1)} %get-tuple-element.9.r_ref, f32[512,128]{1,0:T(8,128)S(1)} %get-tuple-element.10.a_ref, f32[512,128]{1,0:T(8,128)S(1)} %get-tuple-element.11.b_ref, f32[512,128]{1,0:T(8,128)S(1)} %get-tuple-element.12.v_ref, ...), custom_call_target="tpu_custom_call" | custom-call | tf_op jit(solution)/shard_map/pallas_call | solution.py:297

commit v3 on v2

--- a/solution.py
+++ b/solution.py
@@ -10,13 +10,16 @@
 R = 32
 W = 512
 NB = 32
-NS = 4
+NQ = 4
+START = 0
+NS = 8
+PG = 16 // NS
 NV = 6
 
 
-def sweep_kernel(u_hbm, kx_hbm, ky_hbm, g_hbm, r_ref, a_s, b_s, v_s, xf,
+def sweep_kernel(u_hbm, kx_hbm, ky_hbm, g_hbm, r_ref, a_s, b_s, v_s, xf, shift,
                  u_ref, kx_ref, ky_ref, g_ref,
-                 rows_s, cols_s, hrow, hcol, hcor,
+                 rows_s, cols_s, hrow, hcol, hcor, es,
                  ik_s, r_s, msg, inbox, res,
                  ls, hs, hr, ms, mr, rs, rr):
     loads = [pltpu.make_async_copy(src, dst, ls.at[i]) for i, (src, dst) in enumerate(
@@ -32,15 +35,15 @@
         pl.semaphore_signal(barrier, inc=1, device_id=dev, device_id_type=MESH)
 
     barrier = pltpu.get_barrier_semaphore()
-    is_solver = me < NS
+    slot = lax.rem(me + NB - START, NB)
+    is_solver = slot < NS
 
     @pl.when(is_solver)
     def _():
         for k in range(1, NB):
             signal((lax.rem(me + k, NB), gy))
 
-    for dev in ((prev, gy), (nxt, gy), (me, west), (me, east),
-                (prev, west), (prev, east), (nxt, west), (nxt, east)):
+    for dev in ((prev, gy), (nxt, gy), (me, west), (me, east)):
         signal(dev)
 
     loads[0].wait()
@@ -61,7 +64,7 @@
     cols_s[0] = to_east
     cols_s[1] = to_west
 
-    pl.semaphore_wait(barrier, 8 + NS - is_solver.astype(jnp.int32))
+    pl.semaphore_wait(barrier, 4 + NS - is_solver.astype(jnp.int32))
 
     def send(src, dst, i, dev):
         c = pltpu.make_async_remote_copy(src_ref=src, dst_ref=dst, send_sem=hs.at[i], recv_sem=hr.at[i],
@@ -74,15 +77,11 @@
         send(rows_s.at[0], hrow.at[1], 1, (prev, gy)),
         send(cols_s.at[0], hcol.at[0], 2, (me, east)),
         send(cols_s.at[1], hcol.at[1], 3, (me, west)),
-        send(rows_s.at[1, :, pl.ds(384, 128)], hcor.at[0], 4, (nxt, east)),
-        send(rows_s.at[1, :, pl.ds(0, 128)], hcor.at[1], 5, (nxt, west)),
-        send(rows_s.at[0, :, pl.ds(384, 128)], hcor.at[2], 6, (prev, east)),
-        send(rows_s.at[0, :, pl.ds(0, 128)], hcor.at[3], 7, (prev, west)),
     ]
 
     loads[2].wait()
     ik = 1.0 / kx_ref[...].astype(jnp.float32)
-    for q in range(NS):
+    for q in range(NQ):
         ik_s[128 * q:128 * q + 128, :] = ik[:, 128 * q:128 * q + 128]
     a = d = jnp.ones((16, 128), jnp.float32)
     b = c = jnp.zeros((16, 128), jnp.float32)
@@ -97,11 +96,12 @@
         b = b + d * ik
 
     def put(k, value):
-        for q in range(NS):
-            msg[q, 4 * k:4 * k + 4, :] = value[4 * q:4 * q + 4, :]
-
-    for k, value in enumerate((a, b, c, d)):
+        for s in range(NS):
+            msg[s, PG * k:PG * k + PG, :] = value[PG * s:PG * s + PG, :]
+
+    for k, value in enumerate((a, b, c)):
         put(k, value)
+    es[...] = jnp.zeros((6, 16, 128), jnp.float32)
 
     loads[3].wait()
     for h in halos:
@@ -117,15 +117,13 @@
         rest = jnp.zeros((tile.shape[0], W - 128), jnp.float32)
         return jnp.concatenate([rest, tile] if at_end else [tile, rest], axis=1)
 
-    def halo_diff(row, cor_w, cor_e, missing):
-        cw = jnp.where(gy == 0, 0.0, cor_w)
-        ce = jnp.where(gy == 7, 0.0, cor_e)
-        w = jnp.where(lane_p == 0, wide(pltpu.roll(cw, 1, 1), False), pltpu.roll(row, 1, 1))
-        e = jnp.where(lane_p == W - 1, wide(pltpu.roll(ce, 127, 1), True), pltpu.roll(row, W - 1, 1))
+    def halo_diff(row, missing):
+        w = jnp.where(lane_p == 0, 0.0, pltpu.roll(row, 1, 1))
+        e = jnp.where(lane_p == W - 1, 0.0, pltpu.roll(row, W - 1, 1))
         return jnp.where(missing, 0.0, e - w)
 
-    d_prev = halo_diff(hrow[0], hcor[0], hcor[1], me == 0)
-    d_next = halo_diff(hrow[1], hcor[2], hcor[3], me == NB - 1)
+    d_prev = halo_diff(hrow[0], me == 0)
+    d_next = halo_diff(hrow[1], me == NB - 1)
 
     for p in range(PL):
         sl = slice(R * p, R * p + R)
@@ -139,6 +137,11 @@
             ck.append(pltpu.roll(col_w, 112 - m, 1))
             ce.append(pltpu.roll(col_e, 127 - m, 1))
         cw, ck, ce = (jnp.concatenate(t, axis=0) for t in (cw, ck, ce))
+        for k, row in ((0, 0), (1, R - 1)):
+            es[k, p:p + 1, :] = -cw[row:row + 1, :]
+            es[k, 12 + p:13 + p, :] = ce[row:row + 1, :]
+            es[2 + k, p:p + 1, :] = 0.25 * g[row:row + 1, 0:128]
+            es[2 + k, 12 + p:13 + p, :] = 0.25 * g[row:row + 1, W - 128:W]
         uw = jnp.where(lane_w == 0, wide(cw, False), pltpu.roll(u, 1, 1))
         kb = jnp.where(lane_w == 0, wide(ck, False), pltpu.roll(ky, 1, 1))
         ue = jnp.where(lane_w == W - 1, wide(ce, True), pltpu.roll(u, W - 1, 1))
@@ -147,7 +150,7 @@
         dn = jnp.where(row_w == R - 1, d_next[p:p + 1, :], pltpu.roll(dd, R - 1, 0))
         right = u + (ky * (ue - u) - kb * (u - uw)) + g * (dn - up) * 0.25
         r_ref[sl, :] = right
-        for q in range(NS):
+        for q in range(NQ):
             r_s[128 * q + R * p:128 * q + R * p + R, :] = right[:, 128 * q:128 * q + 128]
 
     vx = vf = jnp.zeros((16, 128), jnp.float32)
@@ -156,31 +159,70 @@
         v_s[row, :] = vx
         vf = vf + (vx - r_s[row, :])
         vx = vx + vf * ik_s[row, :]
-    put(4, vx)
-    put(5, vf)
+    put(3, vx)
+    put(4, vf)
+
+    lane_t = lax.broadcasted_iota(jnp.int32, (16, 128), 1)
+    tile_t = lax.broadcasted_iota(jnp.int32, (16, 128), 0) // PL
+
+    def at_edge(k):
+        return ((tile_t == 0) & (lane_t == k)) | ((tile_t == NQ - 1) & (lane_t == (127 + k) % 128))
+
+    edge = jnp.zeros((16, 128), jnp.float32)
+    for k, value in enumerate((es[0], es[1], es[2], es[3], ik_s[pl.ds(R - 1, 16, stride=R), :])):
+        edge = jnp.where(at_edge(k), pltpu.roll(value, k, 1) if k else value, edge)
+    put(5, edge)
 
     def map_copy(s):
         return pltpu.make_async_remote_copy(
             src_ref=msg.at[s],
             dst_ref=inbox.at[me],
-            send_sem=ms.at[s], recv_sem=mr, device_id=(s, gy), device_id_type=MESH)
+            send_sem=ms.at[s], recv_sem=mr, device_id=((START + s) % NB, gy), device_id_type=MESH)
 
     for s in range(NS):
-        @pl.when(me != s)
+        @pl.when(slot != s)
         def _():
             map_copy(s).start()
+
+    corners = [send(hcol, hcor.at[0], 4, (nxt, gy)), send(hcol, hcor.at[1], 5, (prev, gy))]
 
     @pl.when(is_solver)
     def _():
         for s in range(NS):
-            @pl.when(me == s)
+            @pl.when(slot == s)
             def _():
-                inbox[s] = msg[s]
+                inbox[(START + s) % NB] = msg[s]
         part = inbox.at[pl.ds(0, NB - 1)]
         pltpu.make_async_copy(part, part, mr).wait()
 
         def block(p):
-            return [inbox[p, 4 * k:4 * k + 4, :] for k in range(NV)]
+            a, b, c, vx, vf = (inbox[p, PG * k:PG * k + PG, :] for k in range(NV - 1))
+            return a, b, c, (1.0 + b * c) / a, vx, vf
+
+        tile = slot * PG // PL
+        line = jnp.where(tile == 0, 0, jnp.where(tile == NQ - 1, 127, -1))
+
+        @pl.when(line >= 0)
+        def _():
+            here = lax.broadcasted_iota(jnp.int32, (PG, 128), 1) == line
+
+            def edges(p):
+                e = inbox[p, PG * (NV - 1):PG * NV, :]
+                return [e] + [pltpu.roll(e, 128 - k, 1) for k in range(1, 5)]
+
+            before, own = None, edges(0)
+            for p in range(NB):
+                after = edges(p + 1) if p < NB - 1 else None
+                a, b, c, d, vx, vf = block(p)
+                if before is not None:
+                    first = own[2] * before[1]
+                    vx, vf = vx + b * first, vf + d * first
+                if after is not None:
+                    last = own[3] * after[0]
+                    vx, vf = vx - own[4] * last, vf - last
+                inbox[p, PG * 3:PG * 4, :] = jnp.where(here, vx, inbox[p, PG * 3:PG * 4, :])
+                inbox[p, PG * 4:PG * 5, :] = jnp.where(here, vf, inbox[p, PG * 4:PG * 5, :])
+                before, own = own, after
 
         groups = []
         for z in range(8):
@@ -191,7 +233,7 @@
                 b, d = a2 * b + b2 * d, c2 * b + d2 * d
                 vx, vf = a2 * vx + b2 * vf + vx2, c2 * vx + d2 * vf + vf2
             groups.append((a, b, c, d, vx, vf))
-        zero = jnp.zeros((PL, 128), jnp.float32)
+        zero = jnp.zeros((PG, 128), jnp.float32)
         left = [(zero, zero)]
         for z in range(7):
             a, b, c, d, vx, vf = groups[z]
@@ -214,29 +256,47 @@
             f0 = gl * x0 + jl
             for x in range(4):
                 p = 4 * z + x
-                res[p, 0:4, :] = x0
-                res[p, 4:8, :] = f0
+                res[p, 0:PG, :] = x0
+                res[p, PG:2 * PG, :] = f0
                 if x < 3:
                     a, b, c, d, vx, vf = block(p)
                     x0, f0 = a * x0 + b * f0 + vx, c * x0 + d * f0 + vf
 
-        for k in range(1, NB):
-            p = lax.rem(me + k, NS) if k < NS else k
-            pltpu.make_async_remote_copy(
-                src_ref=res.at[p], dst_ref=xf.at[me],
-                send_sem=rs, recv_sem=rr.at[me], device_id=(p, gy), device_id_type=MESH).start()
+        for p in range(NB):
+            @pl.when(me != p)
+            def _():
+                pltpu.make_async_remote_copy(
+                    src_ref=res.at[p], dst_ref=xf.at[slot],
+                    send_sem=rs, recv_sem=rr.at[slot], device_id=(p, gy), device_id_type=MESH).start()
         for s in range(NS):
-            @pl.when(me == s)
+            @pl.when(slot == s)
             def _():
-                xf[s] = res[s]
+                xf[s] = res[(START + s) % NB]
+
+    for corner in corners:
+        corner.wait()
+    for p in range(PL):
+        for k, missing, row, m in ((4, me == 0, 7, 4 * p + 3), (5, me == NB - 1, 0, 4 * p)):
+            w = pltpu.roll(hcor[k - 4, 0], 128 - m, 1) if m else hcor[k - 4, 0]
+            e = pltpu.roll(hcor[k - 4, 1], 127 - m, 1)
+            es[k, p:p + 1, :] = jnp.where(missing | (gy == 0), 0.0, -w[row:row + 1, :])
+            es[k, 12 + p:13 + p, :] = jnp.where(missing | (gy == 7), 0.0, e[row:row + 1, :])
+    first = jnp.where(at_edge(0), -es[2] * es[4], 0.0)
+    last = jnp.where(at_edge(0), es[3] * es[5], 0.0)
+    shift[...] = first
+    for p in range(PL):
+        for q in (0, NQ - 1):
+            ls_q, t = slice(128 * q, 128 * q + 128), PL * q + p
+            r_ref[R * p:R * p + 1, ls_q] = r_ref[R * p:R * p + 1, ls_q] + first[t:t + 1, :]
+            r_ref[R * p + R - 1:R * p + R, ls_q] = r_ref[R * p + R - 1:R * p + R, ls_q] + last[t:t + 1, :]
 
     for s in range(NS):
-        @pl.when(me != s)
+        @pl.when(slot != s)
         def _():
             pltpu.make_async_copy(xf.at[s], xf.at[s], rr.at[s]).wait()
 
     for s in range(NS):
-        @pl.when(me != s)
+        @pl.when(slot != s)
         def _():
             map_copy(s).wait_send()
 
@@ -246,17 +306,18 @@
         pltpu.make_async_copy(part, part, rs).wait()
 
 
-def finish_kernel(r_ref, a_ref, b_ref, v_ref, xf_ref, o_hbm, r_hbm, o_ref, sems):
+def finish_kernel(r_ref, a_ref, b_ref, v_ref, xf_ref, shift_ref, o_hbm, r_hbm, o_ref, sems):
     right = pltpu.make_async_copy(r_ref, r_hbm, sems.at[PL])
     right.start()
     copies = []
     for p in range(PL):
         sl = slice(R * p, R * p + R)
-        for s in range(NS):
-            x0 = xf_ref[s, p:p + 1, :]
-            f0 = xf_ref[s, 4 + p:5 + p, :]
-            ts = slice(128 * s + R * p, 128 * s + R * p + R)
-            o_ref[sl, 128 * s:128 * s + 128] = a_ref[ts, :] * x0 + b_ref[ts, :] * f0 + v_ref[ts, :]
+        for q in range(NQ):
+            s, h = divmod(PL * q + p, PG)
+            x0 = xf_ref[s, h:h + 1, :]
+            f0 = xf_ref[s, PG + h:PG + h + 1, :] - shift_ref[PL * q + p:PL * q + p + 1, :]
+            ts = slice(128 * q + R * p, 128 * q + R * p + R)
+            o_ref[sl, 128 * q:128 * q + 128] = a_ref[ts, :] * x0 + b_ref[ts, :] * f0 + v_ref[ts, :]
         part = pl.ds(R * p, R)
         copies.append(pltpu.make_async_copy(o_ref.at[part], o_hbm.at[part], sems.at[p]))
         copies[-1].start()
@@ -270,7 +331,7 @@
     vmem = pl.BlockSpec(memory_space=pltpu.VMEM)
     hbm = pl.BlockSpec(memory_space=pltpu.HBM)
     f32, bf16 = jnp.float32, jnp.bfloat16
-    tiles = (NS * PL * R, 128)
+    tiles = (NQ * PL * R, 128)
     big = pltpu.VMEM(tiles, f32)
     dma = pltpu.SemaphoreType.DMA
     shape = jax.ShapeDtypeStruct
@@ -279,17 +340,18 @@
     parts = pl.pallas_call(
         sweep_kernel,
         out_shape=(shape(flat, f32), shape(tiles, f32), shape(tiles, f32), shape(tiles, f32),
-                   shape((NS, 8, 128), f32)),
+                   shape((NS, 2 * PG, 128), f32), shape((16, 128), f32)),
         in_specs=[hbm] * 4,
-        out_specs=(vmem,) * 5,
+        out_specs=(vmem,) * 6,
         scratch_shapes=[
             pltpu.VMEM(flat, f32), pltpu.VMEM(flat, bf16), pltpu.VMEM(flat, bf16), pltpu.VMEM(flat, bf16),
             pltpu.VMEM((2, PL, W), f32), pltpu.VMEM((2, 8, 128), f32),
-            pltpu.VMEM((2, PL, W), f32), pltpu.VMEM((2, 8, 128), f32), pltpu.VMEM((4, PL, 128), f32),
+            pltpu.VMEM((2, PL, W), f32), pltpu.VMEM((2, 8, 128), f32), pltpu.VMEM((2, 2, 8, 128), f32),
+            pltpu.VMEM((6, 16, 128), f32),
             big, big,
-            pltpu.VMEM((NS, PL * NV, 128), f32), pltpu.VMEM((NB, PL * NV, 128), f32),
-            pltpu.VMEM((NB, 8, 128), f32),
-            dma((4,)), dma((8,)), dma((8,)), dma((NS,)), dma(()), dma(()), dma((NS,)),
+            pltpu.VMEM((NS, PG * NV, 128), f32), pltpu.VMEM((NB, PG * NV, 128), f32),
+            pltpu.VMEM((NB, 2 * PG, 128), f32),
+            dma((4,)), dma((6,)), dma((6,)), dma((NS,)), dma(()), dma(()), dma((NS,)),
         ],
         compiler_params=pltpu.CompilerParams(
             collective_id=0, has_side_effects=True, vmem_limit_bytes=32 * 2**20),
@@ -297,7 +359,7 @@
     out, rhs = pl.pallas_call(
         finish_kernel,
         out_shape=(shape(flat, f32),) * 2,
-        in_specs=[vmem] * 5,
+        in_specs=[vmem] * 6,
         out_specs=(hbm, hbm),
         scratch_shapes=[pltpu.VMEM(flat, f32), dma((PL + 1,))],
         compiler_params=pltpu.CompilerParams(vmem_limit_bytes=32 * 2**20),

time: 27.3 us -> 24.6 us (0.901)
  the two profiles are of different devices: /device:TPU:1 before, /device:TPU:8 now
where the time goes in v3:
time: 24.6 us; the launch traced here: 24.5 us
  Pallas kernels  23.9 us (97%)
  between operations  0.64 us (3%)
    pallas_call x1, Pallas kernels, shards(): pl.pallas_call(sweep_kernel, out_shape=(shape(flat, f32), shape(tiles, f3...  23.1 us
    pallas_call x1, Pallas kernels, shards(): pl.pallas_call(finish_kernel, out_shape=(shape(flat, f32),) * 2, in_specs...  0.83 us

profile of v3, /device:TPU:8, one launch (start us, length us, event | category | flops | bytes accessed | tf_op | source)
XLA Modules:
  0.0 24.5 jit_solution(13836340156397571228)
XLA Ops:
  0.6 23.1 %shard_map.59 = (f32[128,512]{1,0:T(8,128)S(1)}, f32[512,128]{1,0:T(8,128)S(1)}, f32[512,128]{1,0:T(8,128)S(1)}, f32[512,128]{1,0:T(8,128)S(1)}, f32[8,4,128]{2,1,0:T(4,128)S(1)}, /*index=5*/f32[16,128]{1,0:T(8,128)S(1)}) custom-call(f32[128,512]{1,0:T(8,128)} %bitcast.6, bf16[128,512]{1,0:T(8,128)(2,1)} %bitcast.7, bf16[128,512]{1,0:T(8,128)(2,1)} %bitcast.8, ...), custom_call_target="tpu_custom_call" | custom-call | tf_op jit(solution)/shard_map/pallas_call | solution.py:340
  23.7 0.8 %shard_map.60 = (f32[128,512]{1,0:T(8,128)}, f32[128,512]{1,0:T(8,128)}) custom-call(f32[128,512]{1,0:T(8,128)S(1)} %get-tuple-element.10.r_ref, f32[512,128]{1,0:T(8,128)S(1)} %get-tuple-element.11.a_ref, f32[512,128]{1,0:T(8,128)S(1)} %get-tuple-element.12.b_ref, f32[512,128]{1,0:T(8,128)S(1)} %get-tuple-element.13.v_ref, ...), custom_call_target="tpu_custom_call" | custom-call | tf_op jit(solution)/shard_map/pallas_call | solution.py:359

commit v4 on v3

--- a/solution.py
+++ b/solution.py
@@ -12,15 +12,15 @@
 NB = 32
 NQ = 4
 START = 0
-NS = 8
+NS = 4
 PG = 16 // NS
-NV = 6
+NV = 3
 
 
 def sweep_kernel(u_hbm, kx_hbm, ky_hbm, g_hbm, r_ref, a_s, b_s, v_s, xf, shift,
                  u_ref, kx_ref, ky_ref, g_ref,
                  rows_s, cols_s, hrow, hcol, hcor, es,
-                 ik_s, r_s, msg, inbox, res,
+                 ik_s, r_s, msg, inbox, dmat, gmat, res,
                  ls, hs, hr, ms, mr, rs, rr):
     loads = [pltpu.make_async_copy(src, dst, ls.at[i]) for i, (src, dst) in enumerate(
         ((u_hbm, u_ref), (ky_hbm, ky_ref), (kx_hbm, kx_ref), (g_hbm, g_ref)))]
@@ -95,12 +95,33 @@
         d = d + b
         b = b + d * ik
 
-    def put(k, value):
+    def put(half, k, value):
         for s in range(NS):
-            msg[s, PG * k:PG * k + PG, :] = value[PG * s:PG * s + PG, :]
+            msg[half, s, PG * k:PG * k + PG, :] = value[PG * s:PG * s + PG, :]
+
+    def on_edge(s):
+        return PG * s // PL in (0, NQ - 1)
+
+    def map_copy(half, s):
+        rows = pl.ds(0, PG * (NV if half == 0 or on_edge(s) else NV - 1))
+        return pltpu.make_async_remote_copy(
+            src_ref=msg.at[half, s, rows],
+            dst_ref=inbox.at[half, me, rows],
+            send_sem=ms.at[half, s], recv_sem=mr.at[half], device_id=((START + s) % NB, gy), device_id_type=MESH)
+
+    def send_maps(half):
+        for s in range(NS):
+            @pl.when(slot != s)
+            def _():
+                map_copy(half, s).start()
+
+            @pl.when(slot == s)
+            def _():
+                inbox[half, (START + s) % NB] = msg[half, s]
 
     for k, value in enumerate((a, b, c)):
-        put(k, value)
+        put(0, k, value)
+    send_maps(0)
     es[...] = jnp.zeros((6, 16, 128), jnp.float32)
 
     loads[3].wait()
@@ -159,8 +180,8 @@
         v_s[row, :] = vx
         vf = vf + (vx - r_s[row, :])
         vx = vx + vf * ik_s[row, :]
-    put(3, vx)
-    put(4, vf)
+    put(1, 0, vx)
+    put(1, 1, vf)
 
     lane_t = lax.broadcasted_iota(jnp.int32, (16, 128), 1)
     tile_t = lax.broadcasted_iota(jnp.int32, (16, 128), 0) // PL
@@ -171,89 +192,112 @@
     edge = jnp.zeros((16, 128), jnp.float32)
     for k, value in enumerate((es[0], es[1], es[2], es[3], ik_s[pl.ds(R - 1, 16, stride=R), :])):
         edge = jnp.where(at_edge(k), pltpu.roll(value, k, 1) if k else value, edge)
-    put(5, edge)
-
-    def map_copy(s):
-        return pltpu.make_async_remote_copy(
-            src_ref=msg.at[s],
-            dst_ref=inbox.at[me],
-            send_sem=ms.at[s], recv_sem=mr, device_id=((START + s) % NB, gy), device_id_type=MESH)
-
-    for s in range(NS):
-        @pl.when(slot != s)
-        def _():
-            map_copy(s).start()
+    put(1, 2, edge)
+    send_maps(1)
 
     corners = [send(hcol, hcor.at[0], 4, (nxt, gy)), send(hcol, hcor.at[1], 5, (prev, gy))]
 
     @pl.when(is_solver)
     def _():
-        for s in range(NS):
-            @pl.when(slot == s)
-            def _():
-                inbox[(START + s) % NB] = msg[s]
-        part = inbox.at[pl.ds(0, NB - 1)]
-        pltpu.make_async_copy(part, part, mr).wait()
-
-        def block(p):
-            a, b, c, vx, vf = (inbox[p, PG * k:PG * k + PG, :] for k in range(NV - 1))
-            return a, b, c, (1.0 + b * c) / a, vx, vf
+        def arrived(half, count):
+            part = inbox.at[half, pl.ds(0, NB - 1), pl.ds(0, PG * count)]
+            pltpu.make_async_copy(part, part, mr.at[half]).wait()
+
+        def matrix(p):
+            a, b, c = (inbox[0, p, PG * k:PG * k + PG, :] for k in range(3))
+            return a, b, c, (1.0 + b * c) / a
+
+        def offset(p):
+            return [inbox[1, p, PG * k:PG * k + PG, :] for k in range(2)]
+
+        arrived(0, NV)
+        groups = []
+        for z in range(8):
+            a, b, c, d = matrix(4 * z)
+            dmat[4 * z] = d
+            for x in range(1, 4):
+                a2, b2, c2, d2 = matrix(4 * z + x)
+                dmat[4 * z + x] = d2
+                a, c = a2 * a + b2 * c, c2 * a + d2 * c
+                b, d = a2 * b + b2 * d, c2 * b + d2 * d
+            groups.append((a, b, c, d))
+        zero = jnp.zeros((PG, 128), jnp.float32)
+        gl, gr = zero, zero
+        gls, grs, invl, invr = [zero], [], [], []
+        for z in range(7):
+            a, b, c, d = groups[z]
+            invl.append(1.0 / (a + b * gl))
+            gl = (c + d * gl) * invl[-1]
+            gls.append(gl)
+        a, b, c, d = groups[7]
+        invr.append(1.0 / b)
+        gr = a * invr[0]
+        grs.append(gr)
+        for z in range(6, -1, -1):
+            a, b, c, d = groups[z]
+            invr.insert(0, 1.0 / (d + gr * b))
+            gr = (c + gr * a) * invr[0]
+            grs.insert(0, gr)
+        for z in range(8):
+            gmat[0, z] = gls[z]
+            gmat[1, z] = grs[z]
+            gmat[2, z] = invl[z] if z < 7 else zero
+            gmat[3, z] = invr[z]
+            gmat[4, z] = 1.0 / (gls[z] + grs[z])
 
         tile = slot * PG // PL
         line = jnp.where(tile == 0, 0, jnp.where(tile == NQ - 1, 127, -1))
 
+        @pl.when(line < 0)
+        def _():
+            arrived(1, NV - 1)
+
         @pl.when(line >= 0)
         def _():
+            arrived(1, NV)
             here = lax.broadcasted_iota(jnp.int32, (PG, 128), 1) == line
 
             def edges(p):
-                e = inbox[p, PG * (NV - 1):PG * NV, :]
+                e = inbox[1, p, PG * (NV - 1):PG * NV, :]
                 return [e] + [pltpu.roll(e, 128 - k, 1) for k in range(1, 5)]
 
             before, own = None, edges(0)
             for p in range(NB):
                 after = edges(p + 1) if p < NB - 1 else None
-                a, b, c, d, vx, vf = block(p)
+                vx, vf = offset(p)
+                dx = df = zero
                 if before is not None:
                     first = own[2] * before[1]
-                    vx, vf = vx + b * first, vf + d * first
+                    dx, df = inbox[0, p, PG:2 * PG, :] * first, dmat[p] * first
                 if after is not None:
                     last = own[3] * after[0]
-                    vx, vf = vx - own[4] * last, vf - last
-                inbox[p, PG * 3:PG * 4, :] = jnp.where(here, vx, inbox[p, PG * 3:PG * 4, :])
-                inbox[p, PG * 4:PG * 5, :] = jnp.where(here, vf, inbox[p, PG * 4:PG * 5, :])
+                    dx, df = dx - own[4] * last, df - last
+                inbox[1, p, 0:PG, :] = vx + jnp.where(here, dx, 0.0)
+                inbox[1, p, PG:2 * PG, :] = vf + jnp.where(here, df, 0.0)
                 before, own = own, after
 
-        groups = []
+        def block(p):
+            a, b, c = (inbox[0, p, PG * k:PG * k + PG, :] for k in range(3))
+            return a, b, c, dmat[p], *offset(p)
+
+        sums = []
         for z in range(8):
-            a, b, c, d, vx, vf = block(4 * z)
+            vx, vf = offset(4 * z)
             for x in range(1, 4):
                 a2, b2, c2, d2, vx2, vf2 = block(4 * z + x)
-                a, c = a2 * a + b2 * c, c2 * a + d2 * c
-                b, d = a2 * b + b2 * d, c2 * b + d2 * d
                 vx, vf = a2 * vx + b2 * vf + vx2, c2 * vx + d2 * vf + vf2
-            groups.append((a, b, c, d, vx, vf))
-        zero = jnp.zeros((PG, 128), jnp.float32)
-        left = [(zero, zero)]
+            sums.append((vx, vf))
+        left, right = [zero], []
         for z in range(7):
-            a, b, c, d, vx, vf = groups[z]
-            gl, jl = left[-1]
-            inv = 1.0 / (a + b * gl)
-            gn = (c + d * gl) * inv
-            left.append((gn, jl * inv + vf - gn * vx))
-        a, b, c, d, vx, vf = groups[7]
-        inv = 1.0 / b
-        right = [(a * inv, -vx * inv)]
+            vx, vf = sums[z]
+            left.append(left[-1] * gmat[2, z] + vf - gmat[0, z + 1] * vx)
+        right.append(-sums[7][0] * gmat[3, 7])
         for z in range(6, -1, -1):
-            a, b, c, d, vx, vf = groups[z]
-            gr, jr = right[0]
-            inv = 1.0 / (d + gr * b)
-            right.insert(0, ((c + gr * a) * inv, (jr - vf - gr * vx) * inv))
+            vx, vf = sums[z]
+            right.insert(0, (right[0] - vf - gmat[1, z + 1] * vx) * gmat[3, z])
         for z in range(8):
-            gl, jl = left[z]
-            gr, jr = right[z]
-            x0 = (jr - jl) / (gl + gr)
-            f0 = gl * x0 + jl
+            x0 = (right[z] - left[z]) * gmat[4, z]
+            f0 = gmat[0, z] * x0 + left[z]
             for x in range(4):
                 p = 4 * z + x
                 res[p, 0:PG, :] = x0
@@ -298,7 +342,8 @@
     for s in range(NS):
         @pl.when(slot != s)
         def _():
-            map_copy(s).wait_send()
+            map_copy(0, s).wait_send()
+            map_copy(1, s).wait_send()
 
     @pl.when(is_solver)
     def _():
@@ -349,9 +394,10 @@
             pltpu.VMEM((2, PL, W), f32), pltpu.VMEM((2, 8, 128), f32), pltpu.VMEM((2, 2, 8, 128), f32),
             pltpu.VMEM((6, 16, 128), f32),
             big, big,
-            pltpu.VMEM((NS, PG * NV, 128), f32), pltpu.VMEM((NB, PG * NV, 128), f32),
+            pltpu.VMEM((2, NS, PG * NV, 128), f32), pltpu.VMEM((2, NB, PG * NV, 128), f32),
+            pltpu.VMEM((NB, PG, 128), f32), pltpu.VMEM((5, 8, PG, 128), f32),
             pltpu.VMEM((NB, 2 * PG, 128), f32),
-            dma((4,)), dma((6,)), dma((6,)), dma((NS,)), dma(()), dma(()), dma((NS,)),
+            dma((4,)), dma((6,)), dma((6,)), dma((2, NS)), dma((2,)), dma(()), dma((NS,)),
         ],
         compiler_params=pltpu.CompilerParams(
             collective_id=0, has_side_effects=True, vmem_limit_bytes=32 * 2**20),

time: 24.6 us -> 23.3 us (0.947)
  Pallas kernels: 23.9 us -> 22.6 us
    pallas_call x1, Pallas kernels: 23.1 us -> 21.7 us  [shards(): pl.pallas_call(sweep_kernel, out_shape=(shape(flat, f32), shape(tiles, f3...]
where the time goes in v4:
time: 23.3 us; the launch traced here: 23.2 us
  Pallas kernels  22.6 us (97%)
  between operations  0.64 us (3%)
    pallas_call x1, Pallas kernels, shards(): pl.pallas_call(sweep_kernel, out_shape=(shape(flat, f32), shape(tiles, f3...  21.7 us
    pallas_call x1, Pallas kernels, shards(): pl.pallas_call(finish_kernel, out_shape=(shape(flat, f32),) * 2, in_specs...  0.83 us

profile of v4, /device:TPU:8, one launch (start us, length us, event | category | flops | bytes accessed | tf_op | source)
XLA Modules:
  0.0 23.2 jit_solution(16150980095094572674)
XLA Ops:
  0.6 21.7 %shard_map.59 = (f32[128,512]{1,0:T(8,128)S(1)}, f32[512,128]{1,0:T(8,128)S(1)}, f32[512,128]{1,0:T(8,128)S(1)}, f32[512,128]{1,0:T(8,128)S(1)}, f32[4,8,128]{2,1,0:T(8,128)S(1)}, /*index=5*/f32[16,128]{1,0:T(8,128)S(1)}) custom-call(f32[128,512]{1,0:T(8,128)} %bitcast.6, bf16[128,512]{1,0:T(8,128)(2,1)} %bitcast.7, bf16[128,512]{1,0:T(8,128)(2,1)} %bitcast.8, ...), custom_call_target="tpu_custom_call" | custom-call | tf_op jit(solution)/shard_map/pallas_call | solution.py:385
  22.4 0.8 %shard_map.60 = (f32[128,512]{1,0:T(8,128)}, f32[128,512]{1,0:T(8,128)}) custom-call(f32[128,512]{1,0:T(8,128)S(1)} %get-tuple-element.10.r_ref, f32[512,128]{1,0:T(8,128)S(1)} %get-tuple-element.11.a_ref, f32[512,128]{1,0:T(8,128)S(1)} %get-tuple-element.12.b_ref, f32[512,128]{1,0:T(8,128)S(1)} %get-tuple-element.13.v_ref, ...), custom_call_target="tpu_custom_call" | custom-call | tf_op jit(solution)/shard_map/pallas_call | solution.py:405

commit v5 on v4

v5 whole, which is shorter than its diff:
```python
import jax
import jax.numpy as jnp
from jax import lax
from jax.experimental import pallas as pl
from jax.experimental.pallas import tpu as pltpu
from jax.sharding import PartitionSpec as P

MESH = pl.DeviceIdType.MESH
PL = 4
R = 32
W = 512
NB = 32
NQ = 4
SOLVERS = (0, 5, 2, 7)
NS = 4
PG = 16 // NS
NA = 6
NV = 4


def sweep_kernel(u_hbm, kx_hbm, ky_hbm, g_hbm, r_ref, a_s, b_s, v_s, xf,
                 u_ref, kx_ref, ky_ref, g_ref,
                 cols_s, hcol, es,
                 ik_s, r_s, msg, inbox, msg2, inbox2, dmat, gmat, res,
                 ls, hs, hr, ms, mr, rs, rr):
    loads = [pltpu.make_async_copy(src, dst, ls.at[i]) for i, (src, dst) in enumerate(
        ((u_hbm, u_ref), (ky_hbm, ky_ref), (kx_hbm, kx_ref), (g_hbm, g_ref)))]
    for load in loads:
        load.start()
    me = lax.axis_index("gx")
    gy = lax.axis_index("gy")
    west, east = lax.rem(gy + 7, 8), lax.rem(gy + 1, 8)

    def signal(dev):
        pl.semaphore_signal(barrier, inc=1, device_id=dev, device_id_type=MESH)

    barrier = pltpu.get_barrier_semaphore()
    slot = jnp.int32(NS)
    for s in range(NS):
        slot = jnp.where(me == SOLVERS[s], s, slot)
    is_solver = slot < NS

    @pl.when(is_solver)
    def _():
        for k in range(1, NB):
            signal((lax.rem(me + k, NB), gy))

    for dev in ((me, west), (me, east)):
        signal(dev)

    loads[0].wait()
    loads[1].wait()

    lane = lax.broadcasted_iota(jnp.int32, (8, 128), 1)
    kyf = ky_ref[...].astype(jnp.float32)
    to_east = jnp.zeros((8, 128), jnp.float32)
    to_west = jnp.zeros((8, 128), jnp.float32)
    for m in range(16):
        sl = slice(8 * m, 8 * m + 8)
        to_east = jnp.where(lane == m, pltpu.roll(u_ref[sl, 384:512], (m + 1) % 128, 1), to_east)
        to_east = jnp.where(lane == 16 + m, pltpu.roll(kyf[sl, 384:512], (m + 17) % 128, 1), to_east)
        to_west = jnp.where(lane == m, pltpu.roll(u_ref[sl, 0:128], m, 1) if m else u_ref[sl, 0:128], to_west)
    cols_s[0] = to_east
    cols_s[1] = to_west

    pl.semaphore_wait(barrier, 2 + NS - is_solver.astype(jnp.int32))

    def send(src, dst, i, dev):
        c = pltpu.make_async_remote_copy(src_ref=src, dst_ref=dst, send_sem=hs.at[i], recv_sem=hr.at[i],
                                         device_id=dev, device_id_type=MESH)
        c.start()
        return c

    halos = [send(cols_s.at[0], hcol.at[0], 0, (me, east)), send(cols_s.at[1], hcol.at[1], 1, (me, west))]

    loads[2].wait()
    ik = 1.0 / kx_ref[...].astype(jnp.float32)
    for q in range(NQ):
        ik_s[128 * q:128 * q + 128, :] = ik[:, 128 * q:128 * q + 128]
    a = d = jnp.ones((16, 128), jnp.float32)
    b = c = jnp.zeros((16, 128), jnp.float32)
    for i in range(R):
        row = pl.ds(i, 16, stride=R)
        a_s[row, :] = a
        b_s[row, :] = b
        ik = ik_s[row, :]
        c = c + a
        a = a + c * ik
        d = d + b
        b = b + d * ik

    boxes = ((msg, inbox), (msg2, inbox2))

    def put(half, k, value):
        for s in range(NS):
            boxes[half][0][s, PG * k:PG * k + PG, :] = value[PG * s:PG * s + PG, :]

    def map_copy(half, s):
        source, target = boxes[half]
        return pltpu.make_async_remote_copy(
            src_ref=source.at[s], dst_ref=target.at[me],
            send_sem=ms.at[half, s], recv_sem=mr.at[half], device_id=(SOLVERS[s], gy), device_id_type=MESH)

    def send_maps(half):
        for s in range(NS):
            @pl.when(slot != s)
            def _():
                map_copy(half, s).start()

            @pl.when(slot == s)
            def _():
                boxes[half][1][SOLVERS[s]] = boxes[half][0][s]

    for k, value in enumerate((a, b, c)):
        put(0, k, value)
    loads[3].wait()
    for p in range(PL):
        for k, row in ((0, R * p), (1, R * p + R - 1)):
            line = 0.25 * g_ref[row // 16 * 16:row // 16 * 16 + 16, :].astype(jnp.float32)[row % 16:row % 16 + 1, :]
            for q in range(NQ):
                es[k, PL * q + p:PL * q + p + 1, :] = line[:, 128 * q:128 * q + 128]
    put(0, 3, es[0])
    put(0, 4, es[1])
    put(0, 5, ik_s[pl.ds(R - 1, 16, stride=R), :])
    send_maps(0)

    for h in halos:
        h.wait()

    lane_w = lax.broadcasted_iota(jnp.int32, (R, W), 1)
    row_w = lax.broadcasted_iota(jnp.int32, (R, W), 0)
    col_w = jnp.where(gy == 0, 0.0, hcol[0])
    col_e = jnp.where(gy == 7, 0.0, hcol[1])

    def wide(tile, at_end):
        rest = jnp.zeros((tile.shape[0], W - 128), jnp.float32)
        return jnp.concatenate([rest, tile] if at_end else [tile, rest], axis=1)

    for p in range(PL):
        sl = slice(R * p, R * p + R)
        u = u_ref[sl, :]
        ky = ky_ref[sl, :].astype(jnp.float32)
        g = g_ref[sl, :].astype(jnp.float32)
        cw, ck, ce = [], [], []
        for q in range(4):
            m = 4 * p + q
            cw.append(pltpu.roll(col_w, 128 - m, 1) if m else col_w)
            ck.append(pltpu.roll(col_w, 112 - m, 1))
            ce.append(pltpu.roll(col_e, 127 - m, 1))
        cw, ck, ce = (jnp.concatenate(t, axis=0) for t in (cw, ck, ce))
        uw = jnp.where(lane_w == 0, wide(cw, False), pltpu.roll(u, 1, 1))
        kb = jnp.where(lane_w == 0, wide(ck, False), pltpu.roll(ky, 1, 1))
        ue = jnp.where(lane_w == W - 1, wide(ce, True), pltpu.roll(u, W - 1, 1))
        dd = ue - uw
        for k, row in ((2, 0), (3, R - 1)):
            for q in range(NQ):
                es[k, PL * q + p:PL * q + p + 1, :] = dd[row:row + 1, 128 * q:128 * q + 128]
        up = jnp.where(row_w == 0, 0.0, pltpu.roll(dd, 1, 0))
        dn = jnp.where(row_w == R - 1, 0.0, pltpu.roll(dd, R - 1, 0))
        right = u + (ky * (ue - u) - kb * (u - uw)) + g * (dn - up) * 0.25
        r_ref[sl, :] = right
        for q in range(NQ):
            r_s[128 * q + R * p:128 * q + R * p + R, :] = right[:, 128 * q:128 * q + 128]

    vx = vf = jnp.zeros((16, 128), jnp.float32)
    for i in range(R):
        row = pl.ds(i, 16, stride=R)
        v_s[row, :] = vx
        vf = vf + (vx - r_s[row, :])
        vx = vx + vf * ik_s[row, :]
    put(1, 0, vx)
    put(1, 1, vf)

    put(1, 2, es[2])
    put(1, 3, es[3])
    send_maps(1)

    @pl.when(is_solver)
    def _():
        def arrived(half):
            part = boxes[half][1].at[pl.ds(0, NB - 1)]
            pltpu.make_async_copy(part, part, mr.at[half]).wait()

        def value(half, p, k):
            return boxes[half][1][p, PG * k:PG * k + PG, :]

        def matrix(p):
            a, b, c = (value(0, p, k) for k in range(3))
            return a, b, c, (1.0 + b * c) / a

        def offset(p):
            return [value(1, p, k) for k in range(2)]

        arrived(0)
        groups = []
        for z in range(8):
            a, b, c, d = matrix(4 * z)
            dmat[4 * z] = d
            for x in range(1, 4):
                a2, b2, c2, d2 = matrix(4 * z + x)
                dmat[4 * z + x] = d2
                a, c = a2 * a + b2 * c, c2 * a + d2 * c
                b, d = a2 * b + b2 * d, c2 * b + d2 * d
            groups.append((a, b, c, d))
        zero = jnp.zeros((PG, 128), jnp.float32)
        gl, gr = zero, zero
        gls, grs, invl, invr = [zero], [], [], []
        for z in range(7):
            a, b, c, d = groups[z]
            invl.append(1.0 / (a + b * gl))
            gl = (c + d * gl) * invl[-1]
            gls.append(gl)
        a, b, c, d = groups[7]
        invr.append(1.0 / b)
        gr = a * invr[0]
        grs.append(gr)
        for z in range(6, -1, -1):
            a, b, c, d = groups[z]
            invr.insert(0, 1.0 / (d + gr * b))
            gr = (c + gr * a) * invr[0]
            grs.insert(0, gr)
        for z in range(8):
            gmat[0, z] = gls[z]
            gmat[1, z] = grs[z]
            gmat[2, z] = invl[z] if z < 7 else zero
            gmat[3, z] = invr[z]
            gmat[4, z] = 1.0 / (gls[z] + grs[z])

        arrived(1)
        for p in range(NB):
            first = -value(0, p, 3) * value(1, p - 1, 3) if p > 0 else zero
            last = value(0, p, 4) * value(1, p + 1, 2) if p < NB - 1 else zero
            vx, vf = offset(p)
            inbox2[p, 0:PG, :] = vx - (value(0, p, 1) * first + value(0, p, 5) * last)
            inbox2[p, PG:2 * PG, :] = vf - (dmat[p] * first + last)
            res[p, 2 * PG:3 * PG, :] = first
            res[p, 3 * PG:4 * PG, :] = last

        def block(p):
            a, b, c = (value(0, p, k) for k in range(3))
            return a, b, c, dmat[p], *offset(p)

        sums = []
        for z in range(8):
            vx, vf = offset(4 * z)
            for x in range(1, 4):
                a2, b2, c2, d2, vx2, vf2 = block(4 * z + x)
                vx, vf = a2 * vx + b2 * vf + vx2, c2 * vx + d2 * vf + vf2
            sums.append((vx, vf))
        left, right = [zero], []
        for z in range(7):
            vx, vf = sums[z]
            left.append(left[-1] * gmat[2, z] + vf - gmat[0, z + 1] * vx)
        right.append(-sums[7][0] * gmat[3, 7])
        for z in range(6, -1, -1):
            vx, vf = sums[z]
            right.insert(0, (right[0] - vf - gmat[1, z + 1] * vx) * gmat[3, z])
        for z in range(8):
            x0 = (right[z] - left[z]) * gmat[4, z]
            f0 = gmat[0, z] * x0 + left[z]
            for x in range(4):
                p = 4 * z + x
                res[p, 0:PG, :] = x0
                res[p, PG:2 * PG, :] = f0
                if x < 3:
                    a, b, c, d, vx, vf = block(p)
                    x0, f0 = a * x0 + b * f0 + vx, c * x0 + d * f0 + vf

        for p in range(NB):
            @pl.when(me != p)
            def _():
                pltpu.make_async_remote_copy(
                    src_ref=res.at[p], dst_ref=xf.at[slot],
                    send_sem=rs, recv_sem=rr.at[slot], device_id=(p, gy), device_id_type=MESH).start()
        for s in range(NS):
            @pl.when(slot == s)
            def _():
                xf[s] = res[SOLVERS[s]]

    for s in range(NS):
        @pl.when(slot != s)
        def _():
            pltpu.make_async_copy(xf.at[s], xf.at[s], rr.at[s]).wait()

    for p in range(PL):
        for k, row in ((2, R * p), (3, R * p + R - 1)):
            for q in range(NQ):
                s, h = divmod(PL * q + p, PG)
                at = (slice(row, row + 1), slice(128 * q, 128 * q + 128))
                r_ref[at] = r_ref[at] + xf[s, PG * k + h:PG * k + h + 1, :]

    for s in range(NS):
        @pl.when(slot != s)
        def _():
            map_copy(0, s).wait_send()
            map_copy(1, s).wait_send()

    @pl.when(is_solver)
    def _():
        part = res.at[pl.ds(0, NB - 1)]
        pltpu.make_async_copy(part, part, rs).wait()


def finish_kernel(r_ref, a_ref, b_ref, v_ref, xf_ref, o_hbm, r_hbm, o_ref, sems):
    right = pltpu.make_async_copy(r_ref, r_hbm, sems.at[PL])
    right.start()
    copies = []
    for p in range(PL):
        sl = slice(R * p, R * p + R)
        for q in range(NQ):
            s, h = divmod(PL * q + p, PG)
            x0 = xf_ref[s, h:h + 1, :]
            f0 = xf_ref[s, PG + h:PG + h + 1, :] - xf_ref[s, 2 * PG + h:2 * PG + h + 1, :]
            ts = slice(128 * q + R * p, 128 * q + R * p + R)
            o_ref[sl, 128 * q:128 * q + 128] = a_ref[ts, :] * x0 + b_ref[ts, :] * f0 + v_ref[ts, :]
        part = pl.ds(R * p, R)
        copies.append(pltpu.make_async_copy(o_ref.at[part], o_hbm.at[part], sems.at[p]))
        copies[-1].start()
    for copy in copies:
        copy.wait()
    right.wait()


def shards(state_field, x_coupling, y_coupling, cross_coeff):
    flat = (PL * R, W)
    vmem = pl.BlockSpec(memory_space=pltpu.VMEM)
    hbm = pl.BlockSpec(memory_space=pltpu.HBM)
    f32, bf16 = jnp.float32, jnp.bfloat16
    tiles = (NQ * PL * R, 128)
    big = pltpu.VMEM(tiles, f32)
    dma = pltpu.SemaphoreType.DMA
    shape = jax.ShapeDtypeStruct
    args = [pltpu.with_memory_space_constraint(x.reshape(flat), pltpu.HBM)
            for x in (state_field, x_coupling, y_coupling, cross_coeff)]
    parts = pl.pallas_call(
        sweep_kernel,
        out_shape=(shape(flat, f32), shape(tiles, f32), shape(tiles, f32), shape(tiles, f32),
                   shape((NS, 4 * PG, 128), f32)),
        in_specs=[hbm] * 4,
        out_specs=(vmem,) * 5,
        scratch_shapes=[
            pltpu.VMEM(flat, f32), pltpu.VMEM(flat, bf16), pltpu.VMEM(flat, bf16), pltpu.VMEM(flat, bf16),
            pltpu.VMEM((2, 8, 128), f32), pltpu.VMEM((2, 8, 128), f32), pltpu.VMEM((4, 16, 128), f32),
            big, big,
            pltpu.VMEM((NS, PG * NA, 128), f32), pltpu.VMEM((NB, PG * NA, 128), f32),
            pltpu.VMEM((NS, PG * NV, 128), f32), pltpu.VMEM((NB, PG * NV, 128), f32),
            pltpu.VMEM((NB, PG, 128), f32), pltpu.VMEM((5, 8, PG, 128), f32),
            pltpu.VMEM((NB, 4 * PG, 128), f32),
            dma((4,)), dma((2,)), dma((2,)), dma((2, NS)), dma((2,)), dma(()), dma((NS,)),
        ],
        compiler_params=pltpu.CompilerParams(
            collective_id=0, has_side_effects=True, vmem_limit_bytes=32 * 2**20),
    )(*args)
    out, rhs = pl.pallas_call(
        finish_kernel,
        out_shape=(shape(flat, f32),) * 2,
        in_specs=[vmem] * 5,
        out_specs=(hbm, hbm),
        scratch_shapes=[pltpu.VMEM(flat, f32), dma((PL + 1,))],
        compiler_params=pltpu.CompilerParams(vmem_limit_bytes=32 * 2**20),
    )(*parts)
    return out.reshape(state_field.shape), rhs.reshape(state_field.shape)


def solution(mesh):
    spec = P(None, "gx", "gy")
    return jax.shard_map(shards, mesh=mesh, in_specs=(spec,) * 4, out_specs=(spec, spec), check_vma=False)
```

time: 23.3 us -> 22.6 us (0.970)
  Pallas kernels: 22.6 us -> 21.8 us
    pallas_call x1, Pallas kernels: 21.7 us -> 21 us  [shards(): pl.pallas_call(sweep_kernel, out_shape=(shape(flat, f32), shape(tiles, f3...]
where the time goes in v5:
time: 22.6 us; the launch traced here: 22.5 us
  Pallas kernels  21.8 us (96%)
  between operations  0.64 us (3%)
    pallas_call x1, Pallas kernels, shards(): pl.pallas_call(sweep_kernel, out_shape=(shape(flat, f32), shape(tiles, f3...  21 us
    pallas_call x1, Pallas kernels, shards(): pl.pallas_call(finish_kernel, out_shape=(shape(flat, f32),) * 2, in_specs...  0.83 us

profile of v5, /device:TPU:8, one launch (start us, length us, event | category | flops | bytes accessed | tf_op | source)
XLA Modules:
  0.0 22.5 jit_solution(15285480215830170581)
XLA Ops:
  0.6 21.0 %shard_map.59 = (f32[128,512]{1,0:T(8,128)S(1)}, f32[512,128]{1,0:T(8,128)S(1)}, f32[512,128]{1,0:T(8,128)S(1)}, f32[512,128]{1,0:T(8,128)S(1)}, f32[4,16,128]{2,1,0:T(8,128)S(1)}) custom-call(f32[128,512]{1,0:T(8,128)} %bitcast.6, bf16[128,512]{1,0:T(8,128)(2,1)} %bitcast.7, bf16[128,512]{1,0:T(8,128)(2,1)} %bitcast.8, bf16[128,512]{1,0:T(8,128)(2,1)} %bitcast.9), custom_call_target="tpu_custom_call" | custom-call | tf_op jit(solution)/shard_map/pallas_call | solution.py:335
  21.7 0.8 %shard_map.60 = (f32[128,512]{1,0:T(8,128)}, f32[128,512]{1,0:T(8,128)}) custom-call(f32[128,512]{1,0:T(8,128)S(1)} %get-tuple-element.9.r_ref, f32[512,128]{1,0:T(8,128)S(1)} %get-tuple-element.10.a_ref, f32[512,128]{1,0:T(8,128)S(1)} %get-tuple-element.11.b_ref, f32[512,128]{1,0:T(8,128)S(1)} %get-tuple-element.12.v_ref, ...), custom_call_target="tpu_custom_call" | custom-call | tf_op jit(solution)/shard_map/pallas_call | solution.py:354

commit v6 on v5

--- a/solution.py
+++ b/solution.py
@@ -11,7 +11,6 @@
 W = 512
 NB = 32
 NQ = 4
-SOLVERS = (0, 5, 2, 7)
 NS = 4
 PG = 16 // NS
 NA = 6
@@ -35,9 +34,8 @@
         pl.semaphore_signal(barrier, inc=1, device_id=dev, device_id_type=MESH)
 
     barrier = pltpu.get_barrier_semaphore()
-    slot = jnp.int32(NS)
-    for s in range(NS):
-        slot = jnp.where(me == SOLVERS[s], s, slot)
+    base = NS * lax.rem(gy, 2)
+    slot = jnp.where((me >= base) & (me < base + NS), me - base, NS)
     is_solver = slot < NS
 
     @pl.when(is_solver)
@@ -62,16 +60,6 @@
         to_west = jnp.where(lane == m, pltpu.roll(u_ref[sl, 0:128], m, 1) if m else u_ref[sl, 0:128], to_west)
     cols_s[0] = to_east
     cols_s[1] = to_west
-
-    pl.semaphore_wait(barrier, 2 + NS - is_solver.astype(jnp.int32))
-
-    def send(src, dst, i, dev):
-        c = pltpu.make_async_remote_copy(src_ref=src, dst_ref=dst, send_sem=hs.at[i], recv_sem=hr.at[i],
-                                         device_id=dev, device_id_type=MESH)
-        c.start()
-        return c
-
-    halos = [send(cols_s.at[0], hcol.at[0], 0, (me, east)), send(cols_s.at[1], hcol.at[1], 1, (me, west))]
 
     loads[2].wait()
     ik = 1.0 / kx_ref[...].astype(jnp.float32)
@@ -99,17 +87,20 @@
         source, target = boxes[half]
         return pltpu.make_async_remote_copy(
             src_ref=source.at[s], dst_ref=target.at[me],
-            send_sem=ms.at[half, s], recv_sem=mr.at[half], device_id=(SOLVERS[s], gy), device_id_type=MESH)
+            send_sem=ms.at[half, s], recv_sem=mr.at[half], device_id=(base + s, gy), device_id_type=MESH)
 
     def send_maps(half):
+        for k in (2, 1, 3, 0):
+            far = lax.rem(me + k, NS)
+
+            @pl.when(slot != far)
+            def _():
+                map_copy(half, far).start()
+
         for s in range(NS):
-            @pl.when(slot != s)
-            def _():
-                map_copy(half, s).start()
-
             @pl.when(slot == s)
             def _():
-                boxes[half][1][SOLVERS[s]] = boxes[half][0][s]
+                boxes[half][1][me] = boxes[half][0][s]
 
     for k, value in enumerate((a, b, c)):
         put(0, k, value)
@@ -122,6 +113,17 @@
     put(0, 3, es[0])
     put(0, 4, es[1])
     put(0, 5, ik_s[pl.ds(R - 1, 16, stride=R), :])
+
+    pl.semaphore_wait(barrier, 2 + NS - is_solver.astype(jnp.int32))
+
+    def send(src, dst, i, dev):
+        c = pltpu.make_async_remote_copy(src_ref=src, dst_ref=dst, send_sem=hs.at[i], recv_sem=hr.at[i],
+                                         device_id=dev, device_id_type=MESH)
+        c.start()
+        return c
+
+    halos = [send(cols_s.at[0], hcol.at[0], 0, (me, east)), send(cols_s.at[1], hcol.at[1], 1, (me, west))]
+
     send_maps(0)
 
     for h in halos:
@@ -275,7 +277,7 @@
         for s in range(NS):
             @pl.when(slot == s)
             def _():
-                xf[s] = res[SOLVERS[s]]
+                xf[s] = res[me]
 
     for s in range(NS):
         @pl.when(slot != s)

time: 22.6 us -> 22.2 us (0.982)
  the two profiles are of different devices: /device:TPU:8 before, /device:TPU:32 now
where the time goes in v6:
time: 22.2 us; the launch traced here: 22.1 us
  Pallas kernels  21.4 us (96%)
  between operations  0.64 us (3%)
    pallas_call x1, Pallas kernels, shards(): pl.pallas_call(sweep_kernel, out_shape=(shape(flat, f32), shape(tiles, f3...  20.6 us
    pallas_call x1, Pallas kernels, shards(): pl.pallas_call(finish_kernel, out_shape=(shape(flat, f32),) * 2, in_specs...  0.83 us

profile of v6, /device:TPU:32, one launch (start us, length us, event | category | flops | bytes accessed | tf_op | source)
XLA Modules:
  0.0 22.1 jit_solution(3557048865633869105)
XLA Ops:
  0.6 20.6 %shard_map.59 = (f32[128,512]{1,0:T(8,128)S(1)}, f32[512,128]{1,0:T(8,128)S(1)}, f32[512,128]{1,0:T(8,128)S(1)}, f32[512,128]{1,0:T(8,128)S(1)}, f32[4,16,128]{2,1,0:T(8,128)S(1)}) custom-call(f32[128,512]{1,0:T(8,128)} %bitcast.6, bf16[128,512]{1,0:T(8,128)(2,1)} %bitcast.7, bf16[128,512]{1,0:T(8,128)(2,1)} %bitcast.8, bf16[128,512]{1,0:T(8,128)(2,1)} %bitcast.9), custom_call_target="tpu_custom_call" | custom-call | tf_op jit(solution)/shard_map/pallas_call | solution.py:337
  21.3 0.8 %shard_map.60 = (f32[128,512]{1,0:T(8,128)}, f32[128,512]{1,0:T(8,128)}) custom-call(f32[128,512]{1,0:T(8,128)S(1)} %get-tuple-element.9.r_ref, f32[512,128]{1,0:T(8,128)S(1)} %get-tuple-element.10.a_ref, f32[512,128]{1,0:T(8,128)S(1)} %get-tuple-element.11.b_ref, f32[512,128]{1,0:T(8,128)S(1)} %get-tuple-element.12.v_ref, ...), custom_call_target="tpu_custom_call" | custom-call | tf_op jit(solution)/shard_map/pallas_call | solution.py:356

commit v7 on v6

--- a/solution.py
+++ b/solution.py
@@ -22,29 +22,30 @@
                  cols_s, hcol, es,
                  ik_s, r_s, msg, inbox, msg2, inbox2, dmat, gmat, res,
                  ls, hs, hr, ms, mr, rs, rr):
+    me = lax.axis_index("gx")
+    gy = lax.axis_index("gy")
+    west, east = lax.rem(gy + 7, 8), lax.rem(gy + 1, 8)
+
+    def signal(dev):
+        pl.semaphore_signal(barrier, inc=1, device_id=dev, device_id_type=MESH)
+
+    barrier = pltpu.get_barrier_semaphore()
+    base = NS * lax.rem(gy, 2)
+    slot = jnp.where((me >= base) & (me < base + NS), me - base, NS)
+    is_solver = slot < NS
+
+    for dev in ((me, west), (me, east)):
+        signal(dev)
+
     loads = [pltpu.make_async_copy(src, dst, ls.at[i]) for i, (src, dst) in enumerate(
         ((u_hbm, u_ref), (ky_hbm, ky_ref), (kx_hbm, kx_ref), (g_hbm, g_ref)))]
     for load in loads:
         load.start()
-    me = lax.axis_index("gx")
-    gy = lax.axis_index("gy")
-    west, east = lax.rem(gy + 7, 8), lax.rem(gy + 1, 8)
-
-    def signal(dev):
-        pl.semaphore_signal(barrier, inc=1, device_id=dev, device_id_type=MESH)
-
-    barrier = pltpu.get_barrier_semaphore()
-    base = NS * lax.rem(gy, 2)
-    slot = jnp.where((me >= base) & (me < base + NS), me - base, NS)
-    is_solver = slot < NS
 
     @pl.when(is_solver)
     def _():
         for k in range(1, NB):
             signal((lax.rem(me + k, NB), gy))
-
-    for dev in ((me, west), (me, east)):
-        signal(dev)
 
     loads[0].wait()
     loads[1].wait()
@@ -60,6 +61,16 @@
         to_west = jnp.where(lane == m, pltpu.roll(u_ref[sl, 0:128], m, 1) if m else u_ref[sl, 0:128], to_west)
     cols_s[0] = to_east
     cols_s[1] = to_west
+
+    pl.semaphore_wait(barrier, 2 + NS - is_solver.astype(jnp.int32))
+
+    def send(src, dst, i, dev):
+        c = pltpu.make_async_remote_copy(src_ref=src, dst_ref=dst, send_sem=hs.at[i], recv_sem=hr.at[i],
+                                         device_id=dev, device_id_type=MESH)
+        c.start()
+        return c
+
+    halos = [send(cols_s.at[0], hcol.at[0], 0, (me, east)), send(cols_s.at[1], hcol.at[1], 1, (me, west))]
 
     loads[2].wait()
     ik = 1.0 / kx_ref[...].astype(jnp.float32)
@@ -113,16 +124,6 @@
     put(0, 3, es[0])
     put(0, 4, es[1])
     put(0, 5, ik_s[pl.ds(R - 1, 16, stride=R), :])
-
-    pl.semaphore_wait(barrier, 2 + NS - is_solver.astype(jnp.int32))
-
-    def send(src, dst, i, dev):
-        c = pltpu.make_async_remote_copy(src_ref=src, dst_ref=dst, send_sem=hs.at[i], recv_sem=hr.at[i],
-                                         device_id=dev, device_id_type=MESH)
-        c.start()
-        return c
-
-    halos = [send(cols_s.at[0], hcol.at[0], 0, (me, east)), send(cols_s.at[1], hcol.at[1], 1, (me, west))]
 
     send_maps(0)
 

time: 22.2 us -> 21.9 us (0.986)
  the two profiles are of different devices: /device:TPU:32 before, /device:TPU:8 now
where the time goes in v7:
time: 21.9 us; the launch traced here: 21.7 us
  Pallas kernels  21 us (96%)
  between operations  0.64 us (3%)
    pallas_call x1, Pallas kernels, shards(): pl.pallas_call(sweep_kernel, out_shape=(shape(flat, f32), shape(tiles, f3...  20.2 us
    pallas_call x1, Pallas kernels, shards(): pl.pallas_call(finish_kernel, out_shape=(shape(flat, f32),) * 2, in_specs...  0.83 us

profile of v7, /device:TPU:8, one launch (start us, length us, event | category | flops | bytes accessed | tf_op | source)
XLA Modules:
  0.0 21.7 jit_solution(6333166128572366466)
XLA Ops:
  0.6 20.2 %shard_map.59 = (f32[128,512]{1,0:T(8,128)S(1)}, f32[512,128]{1,0:T(8,128)S(1)}, f32[512,128]{1,0:T(8,128)S(1)}, f32[512,128]{1,0:T(8,128)S(1)}, f32[4,16,128]{2,1,0:T(8,128)S(1)}) custom-call(f32[128,512]{1,0:T(8,128)} %bitcast.6, bf16[128,512]{1,0:T(8,128)(2,1)} %bitcast.7, bf16[128,512]{1,0:T(8,128)(2,1)} %bitcast.8, bf16[128,512]{1,0:T(8,128)(2,1)} %bitcast.9), custom_call_target="tpu_custom_call" | custom-call | tf_op jit(solution)/shard_map/pallas_call | solution.py:338
  20.9 0.8 %shard_map.60 = (f32[128,512]{1,0:T(8,128)}, f32[128,512]{1,0:T(8,128)}) custom-call(f32[128,512]{1,0:T(8,128)S(1)} %get-tuple-element.9.r_ref, f32[512,128]{1,0:T(8,128)S(1)} %get-tuple-element.10.a_ref, f32[512,128]{1,0:T(8,128)S(1)} %get-tuple-element.11.b_ref, f32[512,128]{1,0:T(8,128)S(1)} %get-tuple-element.12.v_ref, ...), custom_call_target="tpu_custom_call" | custom-call | tf_op jit(solution)/shard_map/pallas_call | solution.py:357
